TPU v7x, 128 devices: a whole 4x4x4 slice. The times are simulated.
128 devices in a mesh: scene: 8 (over y_hi, x), row: 16 (over z, y_lo, core).
Axes of the slice: x: 4, y: 4 (y_hi: 2, y_lo: 2; y = y_hi * 2 + y_lo), z: 4, core: 2. Of those that a mesh axis runs over, the one named last changes fastest.
Arguments:
- tokens: bfloat16 [8, 224, 14, 1024], P('scene', 'row'), may hold values from -6 to 6
- qkv_weight: bfloat16 [1024, 3072], replicated, may hold values from -0.1875 to 0.1875
- out_weight: bfloat16 [1024, 1024], replicated, may hold values from -0.1875 to 0.1875
- position_bias: float32 [32, 169], replicated, may hold values from -260 to 260
- window_shift: int32 [2], replicated, may hold values from 1 to 6, as said below
- expert_up: bfloat16 [32, 1024, 4096], P('scene', None, 'row'), may hold values from -0.1875 to 0.1875
- expert_down: bfloat16 [32, 4096, 1024], P('scene', 'row'), may hold values from -0.09375 to 0.09375
- expert_choice: int32 [8, 224, 14, 1], P('scene', 'row'), may hold values from 0 to 31; in each aligned block of 196 rows (0 to 195, 196 to 391, ..., all dimensions but the last counted through in order) at most 7 rows name the same one
- combine_weight: float32 [8, 224, 14], P('scene', 'row'), may hold values from 0.2 to 1
- reduce_weight: bfloat16 [4096, 2048], P(None, 'scene'), may hold values from -0.09375 to 0.09375
- merged_grad: bfloat16 [8, 112, 7, 2048], P(None, 'row', None, 'scene'), may hold values from -6 to 6
Outputs:
- merged: bfloat16 [8, 112, 7, 2048], P(None, 'row', None, 'scene')
- tokens_grad: bfloat16 [8, 224, 14, 1024], P('scene', 'row')
- up_grad: float32 [32, 1024, 4096], P('scene', None, 'row')
- down_grad: float32 [32, 4096, 1024], P('scene', 'row')
Inputs may be any that keep to these rules, and one draw needn't show every extreme that they name: `expert_choice`: within the tokens of one device no expert is named by more than 7 tokens, and in every draw some expert is named by exactly 7 tokens of some device. `window_shift`: both shifts lie between 1 and 6, and one of them equals 6.
All inputs are finite; a program needn't handle non-finite values.
Results may differ from a plain program's by a relative error of at most 0.024.
Values may be sent and summed in bfloat16 or wider, within the bound.
A program may use at most 192 MiB of HBM per device.

v0:
```python
import jax
import jax.numpy as jnp
import numpy as np
from jax import lax
from jax.sharding import PartitionSpec as P

WIN = 7


EPSILON = 1e-05


def from_behind(value, axis, steps):
    count = lax.axis_size(axis)
    pairs = [(source, (source + steps) % count) for source in range(count)]
    return lax.ppermute(value, axis, pairs)


def layer_norm(values):
    centre = jnp.mean(values, axis=-1, keepdims=True)
    centred = values - centre
    spread = jnp.mean(centred * centred, axis=-1, keepdims=True)
    return centred * lax.rsqrt(spread + EPSILON)


def norm_grad(values, cotangent):
    _, pullback = jax.vjp(layer_norm, values)
    return pullback(cotangent)[0]


def gelu_exact(values):
    return jax.nn.gelu(values, approximate=False)


def bias_pairs():
    rel_span = 2 * WIN - 1
    window_area = WIN * WIN
    positions = np.arange(window_area)
    pos_y = positions // WIN
    pos_x = positions % WIN
    relative = (pos_y[:, None] - pos_y[None, :] + WIN - 1) * rel_span + (
        pos_x[:, None] - pos_x[None, :] + WIN - 1
    )
    return (relative.reshape(-1)[:, None] == np.arange(rel_span * rel_span)[None, :]).astype(
        np.float32
    )


def region(first_row, row_count, total_rows, shift_amount):
    position = first_row + jnp.arange(row_count, dtype=jnp.int32)
    return jnp.where(
        position < total_rows - WIN, 0, jnp.where(position < total_rows - shift_amount, 1, 2)
    )


def window_attention(
    field, qkv_weight, out_weight, position_bias, row_start, total_rows, shift_row, shift_col
):
    scene_count, row_count, col_count, features = field.shape
    head_count = position_bias.shape[0]
    head_dim = features // head_count
    window_area = WIN * WIN
    win_rows = row_count // WIN
    win_cols = col_count // WIN
    qkv = jnp.dot(
        field.reshape(-1, features), qkv_weight, preferred_element_type=jnp.float32
    ).astype(jnp.bfloat16)
    qkv = qkv.reshape(scene_count, win_rows, WIN, win_cols, WIN, 3, head_count, head_dim)
    qkv = qkv.transpose(0, 1, 3, 2, 4, 5, 6, 7).reshape(
        scene_count, win_rows * win_cols, window_area, 3, head_count, head_dim
    )
    queries = qkv[:, :, :, 0]
    key_rows = qkv[:, :, :, 1]
    value_rows = qkv[:, :, :, 2]
    pairs = jnp.asarray(bias_pairs().T)
    bias_table = jnp.dot(position_bias, pairs, precision=lax.Precision.HIGHEST).reshape(
        head_count, window_area, window_area
    )
    row_labels = region(row_start, row_count, total_rows, shift_row)
    col_labels = region(0, col_count, col_count, shift_col)
    labels = row_labels[:, None] * 3 + col_labels[None, :]
    labels = (
        labels.reshape(win_rows, WIN, win_cols, WIN)
        .transpose(0, 2, 1, 3)
        .reshape(win_rows * win_cols, window_area)
    )
    region_mask = jnp.where(labels[:, :, None] == labels[:, None, :], 0.0, -100.0).astype(
        jnp.float32
    )
    scores = jnp.einsum("snqhd,snkhd->snhqk", queries, key_rows, preferred_element_type=jnp.float32)
    scores = scores * head_dim ** (-0.5) + bias_table[None, None] + region_mask[None, :, None]
    attn_probs = jax.nn.softmax(scores, axis=-1).astype(jnp.bfloat16)
    mixed_heads = jnp.einsum(
        "snhqk,snkhd->snqhd", attn_probs, value_rows, preferred_element_type=jnp.float32
    ).astype(jnp.bfloat16)
    mixed_heads = mixed_heads.reshape(scene_count, win_rows, win_cols, WIN, WIN, features)
    mixed_heads = mixed_heads.transpose(0, 1, 3, 2, 4, 5).reshape(-1, features)
    projected = jnp.dot(mixed_heads, out_weight, preferred_element_type=jnp.float32).astype(
        jnp.bfloat16
    )
    return projected.reshape(scene_count, row_count, col_count, features)


def route_table(choices, expert_total, capacity):
    onehot = (choices[..., None] == jnp.arange(expert_total, dtype=jnp.int32)).astype(jnp.int32)
    rank_in = jnp.cumsum(onehot, axis=-2) - onehot
    slot_index = jnp.sum(rank_in * onehot, axis=-1)
    position = choices * capacity + slot_index
    return (position[..., None] == jnp.arange(expert_total * capacity, dtype=jnp.int32)).astype(
        jnp.bfloat16
    )


def fold_quads(field):
    return jnp.concatenate(
        [field[:, 0::2, 0::2], field[:, 1::2, 0::2], field[:, 0::2, 1::2], field[:, 1::2, 1::2]],
        axis=-1,
    )


def unfold_quads(grads):
    quarters = jnp.split(grads, 4, axis=-1)
    even_rows = jnp.stack([quarters[0], quarters[2]], 3)
    odd_rows = jnp.stack([quarters[1], quarters[3]], 3)
    rebuilt = jnp.stack([even_rows, odd_rows], 2)
    shape_now = rebuilt.shape
    return rebuilt.reshape(shape_now[0], shape_now[1] * 2, shape_now[3] * 2, shape_now[5])


def local(
    tokens,
    qkv_weight,
    out_weight,
    position_bias,
    window_shift,
    expert_up,
    expert_down,
    expert_choice,
    combine_weight,
    reduce_weight,
    merged_grad,
):
    scene_total = lax.axis_size("scene")
    band_total = lax.axis_size("row")
    band_rows = tokens.shape[1]
    strip_cols = tokens.shape[2]
    features = tokens.shape[3]
    height = band_rows * band_total
    tok_rows = band_rows * strip_cols
    local_experts = expert_up.shape[0]
    expert_total = local_experts * scene_total
    capacity = tok_rows // expert_total + 1
    row_start = lax.axis_index("row") * band_rows
    shift_row = window_shift[0]
    shift_col = window_shift[1]

    def pull_forward(field):
        below = from_behind(field[:, : WIN - 1], "row", -1)
        joined = jnp.concatenate([field, below], axis=1)
        moved = lax.dynamic_slice_in_dim(joined, shift_row, band_rows, 1)
        return jnp.roll(moved, -shift_col, axis=2)

    def push_back(field):
        above = from_behind(field[:, band_rows - (WIN - 1) :], "row", 1)
        joined = jnp.concatenate([above, field], axis=1)
        moved = lax.dynamic_slice_in_dim(joined, WIN - 1 - shift_row, band_rows, 1)
        return jnp.roll(moved, shift_col, axis=2)

    def to_owner(slot_rows):
        grouped = slot_rows.reshape(scene_total, local_experts, capacity, features)
        return lax.all_to_all(grouped, "scene", split_axis=0, concat_axis=0, tiled=True)

    def send_out(slot_rows):
        received = to_owner(slot_rows)
        return lax.all_gather(received[None], "row", axis=0, tiled=True)

    def return_rows(summed):
        returned = lax.all_to_all(summed, "scene", split_axis=1, concat_axis=1, tiled=True)
        return returned.reshape(expert_total * capacity, features)

    def send_home(partial_rows):
        summed = lax.psum_scatter(
            partial_rows.astype(jnp.bfloat16), "row", scatter_dimension=0, tiled=True
        )
        return return_rows(summed)

    tokens_f32 = tokens.astype(jnp.float32)
    normed = layer_norm(tokens_f32).astype(jnp.bfloat16)
    shifted = pull_forward(normed)

    def attend(field):
        return window_attention(
            field, qkv_weight, out_weight, position_bias, row_start, height, shift_row, shift_col
        )

    attended, attend_pull = jax.vjp(attend, shifted)
    restored = push_back(attended)
    after_attn = (tokens_f32 + restored.astype(jnp.float32)).astype(jnp.bfloat16)
    second_norm = layer_norm(after_attn.astype(jnp.float32)).astype(jnp.bfloat16)
    routing = route_table(expert_choice.reshape(1, tok_rows), expert_total, capacity)[0]
    slot_rows = jnp.dot(
        routing.T, second_norm.reshape(tok_rows, features), preferred_element_type=jnp.float32
    ).astype(jnp.bfloat16)
    gathered_in = send_out(slot_rows)
    pre_act = jnp.einsum(
        "rsjkc,jch->rsjkh", gathered_in, expert_up, preferred_element_type=jnp.float32
    )
    activated = gelu_exact(pre_act).astype(jnp.bfloat16)
    partial_out = jnp.einsum(
        "rsjkh,jhc->rsjkc", activated, expert_down, preferred_element_type=jnp.float32
    )
    expert_rows = send_home(partial_out)
    expert_tok = jnp.dot(routing, expert_rows, preferred_element_type=jnp.float32)
    gate_scale = combine_weight.reshape(tok_rows, 1)
    block_out = (
        (after_attn.astype(jnp.float32).reshape(tok_rows, features) + gate_scale * expert_tok)
        .astype(jnp.bfloat16)
        .reshape(tokens.shape)
    )
    quartets = fold_quads(block_out)
    merge_norm = layer_norm(quartets.astype(jnp.float32)).astype(jnp.bfloat16)
    merged = jnp.einsum(
        "nabc,cd->nabd",
        lax.all_gather(merge_norm, "scene", axis=0, tiled=True),
        reduce_weight,
        preferred_element_type=jnp.float32,
    ).astype(jnp.bfloat16)
    d_merge_norm = lax.psum_scatter(
        jnp.einsum(
            "nabd,cd->nabc", merged_grad, reduce_weight, preferred_element_type=jnp.float32
        ).astype(jnp.bfloat16),
        "scene",
        scatter_dimension=0,
        tiled=True,
    ).astype(jnp.float32)
    d_block = unfold_quads(norm_grad(quartets.astype(jnp.float32), d_merge_norm))
    d_expert_tok = gate_scale * d_block.reshape(tok_rows, features)
    d_slot = jnp.einsum(
        "tk,tc->kc", routing.astype(jnp.float32), d_expert_tok, precision=lax.Precision.HIGHEST
    ).astype(jnp.bfloat16)
    _, gelu_pull = jax.vjp(gelu_exact, pre_act)
    slot_grads = send_out(d_slot)
    d_full = jnp.einsum(
        "rsjkc,jhc->rsjkh", slot_grads, expert_down, preferred_element_type=jnp.float32
    )
    d_pre = gelu_pull(d_full)[0].astype(jnp.bfloat16)
    down_grad = jnp.einsum(
        "rsjkh,rsjkc->jhc", activated, slot_grads, preferred_element_type=jnp.float32
    )
    up_grad = jnp.einsum("rsjkc,rsjkh->jch", gathered_in, d_pre, preferred_element_type=jnp.float32)
    d_rows = send_home(
        jnp.einsum("rsjkh,jch->rsjkc", d_pre, expert_up, preferred_element_type=jnp.float32)
    )
    d_second = jnp.dot(routing, d_rows, preferred_element_type=jnp.float32).reshape(tokens.shape)
    d_after = d_block + norm_grad(after_attn.astype(jnp.float32), d_second)
    d_attended = pull_forward(d_after.astype(jnp.bfloat16))
    d_shifted = attend_pull(d_attended)[0]
    d_normed = push_back(d_shifted)
    tokens_grad = (d_after + norm_grad(tokens_f32, d_normed.astype(jnp.float32))).astype(
        jnp.bfloat16
    )
    return (merged, tokens_grad, up_grad, down_grad)


def solution(mesh):
    placed = (
        P("scene", "row", None, None),
        P(),
        P(),
        P(),
        P(),
        P("scene", None, "row"),
        P("scene", "row", None),
        P("scene", "row", None, None),
        P("scene", "row", None),
        P(None, "scene"),
        P(None, "row", None, "scene"),
    )
    return jax.shard_map(
        local,
        mesh=mesh,
        in_specs=placed,
        out_specs=(
            P(None, "row", None, "scene"),
            P("scene", "row", None, None),
            P("scene", None, "row"),
            P("scene", "row", None),
        ),
        check_vma=False,
    )
```

profile of v0, /device:TPU:0, one launch (start us, length us, event | category | flops | bytes accessed | tf_op | source)
XLA Modules:
  0.0 852.2 jit_solution(1084590232599589039)
XLA Ops:
  16.0 4.6 collective-permute-start
  52.6 5.6 reshape.850
  74.6 5.8 fusion.134
  100.7 8.7 %collective-permute-done.1 = bf16[1,6,14,1024]{3,0,2,1:T(2,128)(2,1)S(1)} collective-permute-done((bf16[1,6,14,1024]{3,0,2,1:T(2,128)(2,1)S(1)}, bf16[1,6,14,1024]{3,0,2,1:T(2,128)(2,1)S(1)}, u32[]{:S(2)}, u32[]{:S(2)}) %collective-permute-start.1) | collective-permute-done | bytes 172064 | tf_op jit(solution)/shard_map/ppermute | solution.py:16
  126.9 16.4 %all_to_all.20 = bf16[8,4,7,1024]{3,1,2,0:T(4,128)(2,1)} all-to-all(bf16[8,4,7,1024]{3,1,2,0:T(4,128)(2,1)S(1)} %copy.237), channel_id=1, replica_groups=mesh['scene'=8,'row'=16] {'scene'}, dimensions={0} | all-to-all | bytes 917504 | tf_op jit(solution)/shard_map/all_to_all | solution.py:171
  143.8 41.6 %all-gather.8.cloned.1.call-done = bf16[128,4,7,1024]{3,1,2,0:T(4,128)(2,1)} async-done(((bf16[8,4,7,1024]{3,1,2,0:T(4,128)(2,1)}), bf16[128,4,7,1024]{3,1,2,0:T(4,128)(2,1)}) %all-gather.8.cloned.1.call-update) | async-done | bytes 7340048 | tf_op jit(solution)/shard_map/all_gather | solution.py:175
  185.4 15.1 %fusion.24 = (bf16[16,8,4,7,256]{4,1,3,0,2:T(8,128)(2,1)S(1)}, f32[16,8,4,7,256]{4,1,3,0,2:T(8,128)}, f32[4,16,8,7,256]{4,2,3,1,0:T(8,128)}) fusion(bf16[4,1024,256]{2,1,0:T(8,128)(2,1)S(1)} %copy-done, bf16[128,4,7,1024]{3,1,2,0:T(4,128)(2,1)} %all-gather.8.cloned.1.call-done), kind=kOutput, calls=%fused_computation.40 | convolution fusion | flops 1938685952 | bytes 18612224 | tf_op jit(solution)/shard_map/rsjkc,jch->rsjkh/dot_general | solution.py:205
  201.8 5.0 convert_bitcast_fusion.1
  214.7 191.8 %all-reduce.9.cloned.1.call-done = bf16[16,8,4,7,1024]{4,1,3,0,2:T(8,128)(2,1)} async-done(((bf16[16,8,4,7,1024]{4,1,3,0,2:T(8,128)(2,1)}), bf16[16,8,4,7,1024]{4,1,3,0,2:T(8,128)(2,1)}) %all-reduce.9.cloned.1.call-update) | async-done | bytes 7340048
  409.3 6.4 all-to-all-start.1
  419.1 6.5 all-to-all-done.1
  457.5 12.9 %all_to_all.21 = bf16[8,4,7,1024]{3,1,2,0:T(4,128)(2,1)} all-to-all(bf16[8,4,7,1024]{3,1,2,0:T(4,128)(2,1)S(1)} %copy.246), channel_id=1, replica_groups=mesh['scene'=8,'row'=16] {'scene'}, dimensions={0} | all-to-all | bytes 917504 | tf_op jit(solution)/shard_map/all_to_all | solution.py:171
  470.5 45.0 %all-gather.10.cloned.1.call-done = bf16[128,4,7,1024]{3,1,2,0:T(4,128)(2,1)} async-done(((bf16[8,4,7,1024]{3,1,2,0:T(4,128)(2,1)}), bf16[128,4,7,1024]{3,1,2,0:T(4,128)(2,1)}) %all-gather.10.cloned.1.call-update) | async-done | bytes 7340048 | tf_op jit(solution)/shard_map/all_gather | solution.py:175
  515.5 9.4 %fusion.21 = bf16[16,8,4,7,256]{4,1,3,0,2:T(8,128)(2,1)S(1)} fusion(f32[16,8,4,7,256]{4,1,3,0,2:T(8,128)} %get-tuple-element.28, f32[4,16,8,7,256]{4,2,3,1,0:T(8,128)} %get-tuple-element.48, bf16[4,256,1024]{2,1,0:T(8,128)(2,1)} %param.20, bf16[128,4,7,1024]{3,1,2,0:T(4,128)(2,1)} %all-gather.10.cloned.1.call-done), kind=kOutput, calls=%fused_computation.32 | convolution fusion | flops 1891893248 | bytes 18612224 | tf_op jit(solution)/shard_map/rsjkc,jhc->rsjkh/dot_general | solution.py:243
  526.1 5.1 convert_bitcast_fusion
  533.2 197.6 %all-reduce.11.cloned.1.call-done = bf16[16,8,4,7,1024]{4,1,3,0,2:T(8,128)(2,1)} async-done(((bf16[16,8,4,7,1024]{4,1,3,0,2:T(8,128)(2,1)}), bf16[16,8,4,7,1024]{4,1,3,0,2:T(8,128)(2,1)}) %all-reduce.11.cloned.1.call-update) | async-done | bytes 7340048
  733.8 6.4 all-to-all-start.3
  740.2 4.8 fusion.66
  763.1 9.9 %fusion.38 = f32[4,256,1024]{2,1,0:T(8,128)} fusion(bf16[16,8,4,7,256]{4,1,3,0,2:T(8,128)(2,1)S(1)} %copy-done.19, bf16[128,4,7,1024]{3,1,2,0:T(4,128)(2,1)} %all-gather.10.cloned.1.call-done), kind=kOutput, calls=%fused_computation.60 | convolution fusion | flops 1879048192 | bytes 13369344 | tf_op jit(solution)/shard_map/rsjkh,rsjkc->jhc/dot_general | solution.py:247
  795.1 9.7 %copy.259 = bf16[1,4,49,3,32,32]{5,4,3,2,1,0:T(8,128)(2,1)} copy(bf16[1,4,49,3,32,32]{2,5,4,1,3,0:T(8,128)(2,1)} %pad_add_fusion) | data formatting | bytes 2408448 | tf_op jit(solution)/shard_map/transpose(jvp())/add_any | solution.py:72
  804.8 5.9 copy.260
  810.7 6.7 reshape.878
  817.4 4.9 convolution_convert_fusion.9
  823.4 10.6 %fusion.41 = f32[4,1024,256]{2,1,0:T(8,128)} fusion(bf16[128,4,7,1024]{3,1,2,0:T(4,128)(2,1)} %all-gather.8.cloned.1.call-done, bf16[16,8,4,7,256]{4,1,3,0,2:T(8,128)(2,1)} %copy-done.20), kind=kOutput, calls=%fused_computation.61 | convolution fusion | flops 1879048192 | bytes 13369344 | tf_op jit(solution)/shard_map/rsjkc,rsjkh->jch/dot_general | solution.py:250
  (236 shorter events, 193.5 us)
Async XLA Ops:
  8.0 177.4 %copy-start = (bf16[4,1024,256]{2,1,0:T(8,128)(2,1)S(1)}, bf16[4,1024,256]{2,1,0:T(8,128)(2,1)}, u32[]{:S(2)}) copy-start(bf16[4,1024,256]{2,1,0:T(8,128)(2,1)} %param.19) | copy-start | bytes 6291460
  8.0 177.4 %all-gather.8.cloned.1.call-start = ((), (), s32[]{:S(2)}) async-start(), calls=%async_computation.7 | async-start | bytes 7798784 | tf_op jit(solution)/shard_map/all_gather | solution.py:175
  16.0 26.6 %collective-permute-start = (bf16[1,6,14,1024]{3,0,2,1:T(2,128)(2,1)}, bf16[1,6,14,1024]{3,0,2,1:T(2,128)(2,1)S(1)}, u32[]{:S(2)}, u32[]{:S(2)}) collective-permute-start(bf16[1,6,14,1024]{3,0,2,1:T(2,128)(2,1)} %slice.64), channel_id=1, source_target_pairs={{0,15},{1,0},{2,1},{3,2},{4,3},{5,4},{6,5},{7,6},{8,7},{9,8},{10,9... | collective-permute-start | bytes 516104 | tf_op jit(solution)/shard_map/ppermute | solution.py:16
  64.3 10.2 %copy-start.25 = (f32[4,49,49]{1,2,0:T(8,128)S(1)}, f32[4,49,49]{1,2,0:T(8,128)}, u32[]{:S(2)}) copy-start(f32[4,49,49]{1,2,0:T(8,128)} %compare_select_fusion) | copy-start | bytes 115252
  93.5 17.4 %copy-start.2 = (bf16[1,14,14,1024]{3,2,1,0:T(8,128)(2,1)S(1)}, bf16[1,14,14,1024]{3,2,1,0:T(8,128)(2,1)}, u32[]{:S(2)}) copy-start(bf16[1,14,14,1024]{3,2,1,0:T(8,128)(2,1)} %param.14) | copy-start | bytes 1204228
  100.4 9.1 %collective-permute-start.1 = (bf16[1,6,14,1024]{3,0,2,1:T(2,128)(2,1)S(1)}, bf16[1,6,14,1024]{3,0,2,1:T(2,128)(2,1)S(1)}, u32[]{:S(2)}, u32[]{:S(2)}) collective-permute-start(bf16[1,6,14,1024]{3,0,2,1:T(2,128)(2,1)S(1)} %slice.68), channel_id=1, source_target_pairs={{0,1},{1,2},{2,3},{3,4},{4,5},{5,6},{6,7},{7,8},{8,9},{9,10},{10,1... | collective-permute-start | bytes 516104 | tf_op jit(solution)/shard_map/ppermute | solution.py:16
  100.7 327.0 %copy-start.35 = (s32[196]{0:T(256)}, s32[196]{0:T(256)S(1)}, u32[]{:S(2)}) copy-start(s32[196]{0:T(256)S(1)} %multiply_add_fusion.3) | copy-start | bytes 2356
  143.3 263.1 %all-reduce.9.cloned.1.call-start = ((), (), s32[]{:S(2)}) async-start(), calls=%async_computation.9 | async-start | bytes 14680064
  185.4 16.4 %copy-start.16 = (bf16[4,256,1024]{2,1,0:T(8,128)(2,1)S(1)}, bf16[4,256,1024]{2,1,0:T(8,128)(2,1)}, u32[]{:S(2)}) copy-start(bf16[4,256,1024]{2,1,0:T(8,128)(2,1)} %param.20) | copy-start | bytes 6291460
  206.8 236.0 %reduce-scatter.4.cloned.1.call-start = ((), (), s32[]{:S(2)}) async-start(), calls=%async_computation.6 | async-start | bytes 4128768 | tf_op jit(solution)/shard_map/reduce_scatter | solution.py:228
  214.0 202.0 %copy-start.39 = (f32[1,14,14]{2,0,1:T(1,128)S(1)}, f32[1,14,14]{2,0,1:T(1,128)}, u32[]{:S(2)}) copy-start(f32[1,14,14]{2,0,1:T(1,128)} %param.22) | copy-start | bytes 2356
  409.3 16.4 %all-to-all-start.1 = ((bf16[1,8,4,7,1024]{4,2,3,0,1:T(4,128)(2,1)}), bf16[1,8,4,7,1024]{4,2,3,0,1:T(4,128)(2,1)}, u32[]{:S(2)}, u32[]{:S(2)}) async-start(bf16[1,8,4,7,1024]{4,2,3,0,1:T(4,128)(2,1)} %copy.240), calls=%async_computation.1 | async-start | bytes 917504 | tf_op jit(solution)/shard_map/all_to_all | solution.py:178
  415.7 99.8 %all-gather.10.cloned.1.call-start = ((), (), s32[]{:S(2)}) async-start(), calls=%async_computation.8 | async-start | bytes 7798784 | tf_op jit(solution)/shard_map/all_gather | solution.py:175
  470.4 260.5 %all-reduce.11.cloned.1.call-start = ((), (), s32[]{:S(2)}) async-start(), calls=%async_computation.10 | async-start | bytes 14680064
  531.2 208.9 %all-gather.6.cloned.1.call-start = ((), (), s32[]{:S(2)}) async-start(), calls=%async_computation.5 | async-start | bytes 4128768 | tf_op jit(solution)/shard_map/all_gather | solution.py:224
  533.2 226.6 %copy-start.10 = (f32[1,7,2,7,2,1024]{5,0,4,3,2,1:T(1,128)}, f32[1,7,2,7,2,1024]{5,0,4,3,2,1:T(1,128)S(1)}, u32[]{:S(2)}) copy-start(f32[1,7,2,7,2,1024]{5,0,4,3,2,1:T(1,128)S(1)} %copy.243) | copy-start | bytes 2408452
  733.8 16.3 %all-to-all-start.3 = ((bf16[1,8,4,7,1024]{4,2,3,0,1:T(4,128)(2,1)}), bf16[1,8,4,7,1024]{4,2,3,0,1:T(4,128)(2,1)S(1)}, u32[]{:S(2)}, u32[]{:S(2)}) async-start(bf16[1,8,4,7,1024]{4,2,3,0,1:T(4,128)(2,1)} %copy.249), calls=%async_computation.4 | async-start | bytes 917504 | tf_op jit(solution)/shard_map/all_to_all | solution.py:178
  745.0 10.4 %copy-start.31 = (f32[14,14]{1,0:T(8,128)S(1)}, f32[14,14]{1,0:T(8,128)}, u32[]{:S(2)}) copy-start(f32[14,14]{1,0:T(8,128)} %copy-done.30) | copy-start | bytes 2356
  753.7 9.5 %copy-start.19 = (bf16[16,8,4,7,256]{4,1,3,0,2:T(8,128)(2,1)S(1)}, bf16[16,8,4,7,256]{4,1,3,0,2:T(8,128)(2,1)}, u32[]{:S(2)}) copy-start(bf16[16,8,4,7,256]{4,1,3,0,2:T(8,128)(2,1)} %copy-done.18) | copy-start | bytes 5505028
  759.9 13.2 %copy-start.28 = (f32[14,14]{1,0:T(8,128)}, f32[14,14]{1,0:T(8,128)S(1)}, u32[]{:S(2)}) copy-start(f32[14,14]{1,0:T(8,128)S(1)} %negate_multiply_fusion.2) | copy-start | bytes 2356
  761.2 11.9 %collective-permute-start.2 = (bf16[1,6,14,1024]{3,0,2,1:T(2,128)(2,1)S(1)}, bf16[1,6,14,1024]{3,0,2,1:T(2,128)(2,1)S(1)}, u32[]{:S(2)}, u32[]{:S(2)}) collective-permute-start(bf16[1,6,14,1024]{3,0,2,1:T(2,128)(2,1)S(1)} %slice.71), channel_id=1, source_target_pairs={{0,15},{1,0},{2,1},{3,2},{4,3},{5,4},{6,5},{7,6},{8,7},{9,8},{10,9... | collective-permute-start | bytes 516104 | tf_op jit(solution)/shard_map/ppermute | solution.py:16
  823.1 12.5 %copy-start.3 = (bf16[1,14,14,1024]{3,2,1,0:T(8,128)(2,1)S(1)}, bf16[1,14,14,1024]{3,2,1,0:T(8,128)(2,1)}, u32[]{:S(2)}) copy-start(bf16[1,14,14,1024]{3,2,1,0:T(8,128)(2,1)} %param.14) | copy-start | bytes 1204228
  823.1 12.4 %copy-start.24 = (f32[14,14]{1,0:T(8,128)S(1)}, f32[14,14]{1,0:T(8,128)}, u32[]{:S(2)}) copy-start(f32[14,14]{1,0:T(8,128)} %copy-done.23) | copy-start | bytes 2356
  823.1 11.0 %collective-permute-start.3 = (bf16[1,6,14,1024]{3,0,2,1:T(2,128)(2,1)S(1)}, bf16[1,6,14,1024]{3,0,2,1:T(2,128)(2,1)S(1)}, u32[]{:S(2)}, u32[]{:S(2)}) collective-permute-start(bf16[1,6,14,1024]{3,0,2,1:T(2,128)(2,1)S(1)} %slice.72), channel_id=1, source_target_pairs={{0,1},{1,2},{2,3},{3,4},{4,5},{5,6},{6,7},{7,8},{8,9},{9,10},{10,1... | collective-permute-start | bytes 516104 | tf_op jit(solution)/shard_map/ppermute | solution.py:16
  (31 other events, 132.5 us)
Sparse Core Ops, SparseCore 0:
  143.4 41.9 all-gather.7
  206.9 199.4 all-reduce.8
  470.5 44.9 all-gather.9
  531.4 199.4 all-reduce.10
Sparse Core Ops, SparseCore 1:
  214.1 103.6 reduce-scatter.3
  534.9 71.9 all-gather.5
where the time goes:
time: 859 us; the launch traced here: 852 us
  waiting for transfers between devices  496 us (58%)
  local copies, waits for them, and re-layouts  120 us (14%)
  matrix products  101 us (12%)
  other arithmetic  62 us (7%)
  blocking collectives  29.3 us (3%)
  between operations  22 us (3%)
  starting transfers between devices  21 us (2%)
    unnamed x8, waiting for transfers between devices  390 us
    all_gather x2, waiting for transfers between devices, send_out(): return lax.all_gather(received[None], 'row', axis=0, tiled=True)  86.7 us
    all_to_all x2, blocking collectives, to_owner(): lax.all_to_all(grouped, 'scene', split_axis=0, concat_axis=0, tiled=True)  29.3 us
    unnamed x94, local copies, waits for them, and re-layouts  23.2 us
  transfers between devices with their start and end apart: 12, of which 7 were waited for; matrix products, arithmetic and copies ran while one was open for 9% of the time, Pallas kernels for 0%

commit v1 on v0

v1 whole, which is shorter than its diff:
```python
import functools

import jax
import jax.numpy as jnp
import numpy as np
from jax import lax
from jax.experimental import pallas as pl
from jax.experimental.pallas import tpu as pltpu
from jax.sharding import PartitionSpec as P

MESH = pl.DeviceIdType.MESH
F32 = jnp.float32
BF = jnp.bfloat16
EPS = 1e-5
C = 1024
HC = C // 2
TOK = 196
TP = 208
HALO = 96
GRP = 256
NEG = -1e30
VMEM_BIG = 56 * 1024 * 1024
VM = pl.BlockSpec(memory_space=pltpu.VMEM)
SM = pl.BlockSpec(memory_space=pltpu.SMEM)
HB = pl.BlockSpec(memory_space=pl.ANY)


def sds(shape, dtype):
    return jax.ShapeDtypeStruct(shape, dtype)


def params(**kw):
    return pltpu.CompilerParams(vmem_limit_bytes=VMEM_BIG, **kw)


def cost(flops, nbytes):
    return pl.CostEstimate(flops=flops, bytes_accessed=nbytes, transcendentals=0)


def dot(a, b, da=1, db=0):
    return lax.dot_general(a, b, (((da,), (db,)), ((), ())), preferred_element_type=F32)


def iota(shape, dim):
    return lax.broadcasted_iota(jnp.int32, shape, dim)


def norm_parts(values):
    centre = jnp.mean(values, axis=-1, keepdims=True)
    centred = values - centre
    spread = jnp.mean(centred * centred, axis=-1, keepdims=True)
    scale = lax.rsqrt(spread + EPS)
    return centred * scale, scale


def norm_back(values, cot):
    unit, scale = norm_parts(values)
    mean_cot = jnp.mean(cot, axis=-1, keepdims=True)
    mean_dot = jnp.mean(cot * unit, axis=-1, keepdims=True)
    return scale * (cot - mean_cot - unit * mean_dot)


def split3(values):
    high = values.astype(BF)
    rest = values - high.astype(F32)
    mid = rest.astype(BF)
    low = (rest - mid.astype(F32)).astype(BF)
    return high, mid, low


def place_of(tok, r, c):
    rho = (tok * 4682) >> 16
    gam = tok - 14 * rho
    i = rho - r
    i = jnp.where(i < 0, i + 14, i)
    j = gam - c
    j = jnp.where(j < 0, j + 14, j)
    a = jnp.where(i >= 7, 1, 0)
    b = jnp.where(j >= 7, 1, 0)
    return i, j, a, b


def pos_of(tok, r, c):
    i, j, a, b = place_of(tok, r, c)
    return (i - 7 * a) * 7 + (j - 7 * b)


def group_of(tok, r, c, last):
    i, j, a, b = place_of(tok, r, c)
    la = jnp.where(i >= 7, jnp.where(i < 14 - r, 1, 2), 0) * last
    lb = jnp.where(j >= 7, jnp.where(j < 14 - c, 1, 2), 0)
    return a * 2 + b, la * 3 + lb


def pack_rows(low, high, blocks):
    return jnp.concatenate([low.reshape(blocks, 8, HC), high.reshape(blocks, 8, HC)], axis=1).astype(BF)


def unpack_rows(packed, blocks):
    wide = packed.astype(F32)
    low = wide[:, :8, :].reshape(blocks * 8, HC)
    high = wide[:, 8:, :].reshape(blocks * 8, HC)
    return low, high


def attn_fwd(scal, x, halo, wq, wk, wv, wo, bias, att, q_out, k_out, v_out, p_out, normed, mask, ecol, erow, acc):
    g = pl.program_id(0)

    @pl.when(g == 0)
    def _():
        r, c, last = scal[0], scal[1], scal[2]
        own = x[:HALO, :].astype(F32)
        top = jnp.where(iota((HALO, C), 0) < 14 * r, halo[...].astype(F32), own)
        normed[:HALO, :] = norm_parts(top)[0].astype(BF)
        normed[HALO:, :] = norm_parts(x[HALO:, :].astype(F32))[0].astype(BF)
        tq, tk = iota((TP, TP), 0), iota((TP, TP), 1)
        wq_, lq = group_of(tq, r, c, last)
        wk_, lk = group_of(tk, r, c, last)
        open_ = jnp.where(lq == lk, 0.0, -100.0)
        seen = jnp.where(wq_ == wk_, open_, NEG)
        mask[...] = jnp.where(tk < TOK, seen, NEG)
        row_pos = pos_of(iota((TP, 192), 0), r, c)
        erow[...] = jnp.where(row_pos == (iota((TP, 192), 1) & 63), 1.0, 0.0).astype(BF)
        col_pos = pos_of(iota((192, TP), 1), r, c)
        ecol[...] = jnp.where(col_pos == (iota((192, TP), 0) & 63), 1.0, 0.0).astype(BF)
        acc[...] = jnp.zeros_like(acc)

    n = normed[...]
    q = dot(n, wq[...]).astype(BF)
    k = dot(n, wk[...]).astype(BF)
    v = dot(n, wv[...]).astype(BF)
    q_out[...] = q
    k_out[...] = k
    v_out[...] = v
    wide = dot(jnp.concatenate(split3(bias[...].reshape(8 * 64, 64)), axis=1), ecol[...])
    w_hi, w_mid, w_lo = split3(wide)
    lane_head = iota((TP, GRP), 1) >> 5
    mixed = jnp.zeros((TP, GRP), F32)
    q32 = q.astype(F32)
    for h in range(8):
        mine = lane_head == h
        qm = jnp.where(mine, q32, 0.0).astype(BF)
        s = dot(qm, k, 1, 1) * (32.0 ** -0.5)
        part = slice(h * 64, h * 64 + 64)
        s = s + dot(erow[...], jnp.concatenate([w_hi[part], w_mid[part], w_lo[part]], axis=0)) + mask[...]
        e = jnp.exp(s - jnp.max(s, axis=-1, keepdims=True))
        p = (e / jnp.sum(e, axis=-1, keepdims=True)).astype(BF)
        p_out[h * TP:(h + 1) * TP, :] = p
        mixed = jnp.where(mine, dot(p, v), mixed)
    acc[...] += dot(mixed.astype(BF), wo[...])

    @pl.when(g == 3)
    def _():
        att[...] = acc[...].astype(BF)


def attn_bwd(scal, own, halo, wq, wk, wv, wo, q_in, k_in, v_in, p_in, d_shift, d_att, acc):
    g = pl.program_id(0)

    @pl.when(g == 0)
    def _():
        top = jnp.where(iota((HALO, C), 0) < 14 * scal[0], halo[...].astype(F32), own[:HALO, :].astype(F32))
        d_att[:HALO, :] = top.astype(BF)
        d_att[HALO:, :] = own[HALO:, :]
        acc[...] = jnp.zeros_like(acc)

    q, k, v = q_in[...], k_in[...], v_in[...]
    d_mixed = dot(d_att[...], wo[...], 1, 1).astype(BF).astype(F32)
    q32 = q.astype(F32)
    lane_head = iota((TP, GRP), 1) >> 5
    dq = jnp.zeros((TP, GRP), F32)
    dk = jnp.zeros((TP, GRP), F32)
    dv = jnp.zeros((TP, GRP), F32)
    for h in range(8):
        mine = lane_head == h
        dm = jnp.where(mine, d_mixed, 0.0).astype(BF)
        qm = jnp.where(mine, q32, 0.0).astype(BF)
        p = p_in[h * TP:(h + 1) * TP, :]
        p32 = p.astype(F32)
        dp = dot(dm, v, 1, 1).astype(BF).astype(F32)
        ds = p32 * (dp - jnp.sum(dp * p32, axis=-1, keepdims=True)) * (32.0 ** -0.5)
        ds = ds.astype(BF)
        dq = jnp.where(mine, dot(ds, k), dq)
        dk = dk + dot(ds, qm, 0, 0)
        dv = dv + dot(p, dm, 0, 0)
    acc[...] += dot(dq.astype(BF), wq[...], 1, 1) + dot(dk.astype(BF), wk[...], 1, 1) + dot(dv.astype(BF), wv[...], 1, 1)

    @pl.when(g == 3)
    def _():
        d_shift[...] = acc[...].astype(BF)


def route(scal, x, att, halo, choice_col, choice_row, after_out, slots, table_out):
    r = scal[0]
    top = jnp.where(iota((HALO, C), 0) < 14 * r, halo[...].astype(F32), att[:HALO, :].astype(F32))
    after_out[:HALO, :] = (x[:HALO, :].astype(F32) + top).astype(BF)
    after_out[HALO:, :] = (x[HALO:, :].astype(F32) + att[HALO:, :].astype(F32)).astype(BF)
    after = after_out[...].astype(F32)
    n2 = norm_parts(after)[0].astype(BF)
    col = choice_col[...]
    same = jnp.where(col == choice_row[...], 1.0, 0.0)
    same = jnp.where(iota((TP, TP), 1) < iota((TP, TP), 0), same, 0.0)
    rank = jnp.sum(same, axis=1, keepdims=True).astype(jnp.int32)
    table = jnp.where(col * 8 + rank == iota((TP, 256), 1), 1.0, 0.0).astype(BF)
    table_out[...] = table
    slots[...] = pack_rows(dot(table, n2[:, :HC], 0, 0), dot(table, n2[:, HC:], 0, 0), 32)


def quad_table():
    row = iota((256, TP), 0)
    tok = iota((256, TP), 1)
    q = row >> 6
    n = row & 63
    a = (n * 9363) >> 16
    b = n - 7 * a
    want = (2 * a + (q & 1)) * 14 + 2 * b + (q >> 1)
    hit = jnp.where(want == tok, 1.0, 0.0)
    return jnp.where(n < 49, hit, 0.0).astype(BF)


def gathered(ret, table):
    low, high = unpack_rows(ret[0].astype(F32) + ret[1].astype(F32), 32)
    return jnp.concatenate([dot(table, low.astype(BF)), dot(table, high.astype(BF))], axis=1)


def merge_mid(after, ret, table_in, gate_in, parts, mn_out, d_block_out, slots, spread):
    table = table_in[...]
    gate = gate_in[...]
    block = (after[...].astype(F32) + gate * gathered(ret, table)).astype(BF)
    perm = quad_table()
    quads = dot(perm, block)
    vals = [quads[64 * q:64 * q + 49, :] for q in range(4)]
    inv = 1.0 / (4 * C)
    centre = sum(jnp.sum(v, axis=-1, keepdims=True) for v in vals) * inv
    cent = [v - centre for v in vals]
    var = sum(jnp.sum(v * v, axis=-1, keepdims=True) for v in cent) * inv
    scale = lax.rsqrt(var + EPS)
    unit = [v * scale for v in cent]
    for q in range(4):
        mn_out[:, q * C:(q + 1) * C] = unit[q].astype(BF)
    cots = []
    for q in range(4):
        tot = parts[0, :, q * C:(q + 1) * C].astype(F32)
        for s in range(1, 8):
            tot = tot + parts[s, :, q * C:(q + 1) * C].astype(F32)
        cots.append(tot)
    mean_cot = sum(jnp.sum(v, axis=-1, keepdims=True) for v in cots) * inv
    mean_dot = sum(jnp.sum(v * u, axis=-1, keepdims=True) for v, u in zip(cots, unit)) * inv
    spread[...] = jnp.zeros_like(spread)
    for q in range(4):
        spread[64 * q:64 * q + 49, :] = scale * (cots[q] - mean_cot - unit[q] * mean_dot)
    high, mid, low = split3(spread[...])
    d_block = dot(perm, high, 0, 0) + dot(perm, mid, 0, 0) + dot(perm, low, 0, 0)
    d_block_out[...] = d_block
    scaled = (gate * d_block).astype(BF)
    slots[...] = pack_rows(dot(table, scaled[:, :HC], 0, 0), dot(table, scaled[:, HC:], 0, 0), 32)


def after_back(after, ret, table, d_block, d_after_out, d_att_out):
    d_second = gathered(ret, table[...])
    d_after = d_block[...] + norm_back(after[...].astype(F32), d_second)
    d_after_out[...] = d_after
    d_att_out[...] = d_after.astype(BF)


def finish(scal, x, d_after, own, halo, out):
    r = scal[0]
    top = jnp.where(iota((HALO, C), 0) < 14 * r, halo[...].astype(F32), own[:HALO, :].astype(F32))
    out[:HALO, :] = (d_after[:HALO, :] + norm_back(x[:HALO, :].astype(F32), top)).astype(BF)
    out[HALO:, :] = (
        d_after[HALO:, :] + norm_back(x[HALO:, :].astype(F32), own[HALO:, :].astype(F32))
    ).astype(BF)


def expert_fwd(slots, *refs):
    ups, downs = refs[:4], refs[4:8]
    flat, act_out, slope_out, packed = refs[8:]
    low, high = unpack_rows(slots[...], 32)
    rows = jnp.concatenate([low, high], axis=1).astype(BF)
    flat[...] = rows
    total = jnp.zeros((256, C), F32)
    for k in range(4):
        pre = dot(rows, ups[k][...])
        cdf = 0.5 * (1.0 + lax.erf(pre * np.float32(2.0 ** -0.5)))
        act = (pre * cdf).astype(BF)
        slope = cdf + pre * jnp.exp(-0.5 * pre * pre) * np.float32((2.0 * np.pi) ** -0.5)
        act_out[:, k * 256:(k + 1) * 256] = act
        slope_out[:, k * 256:(k + 1) * 256] = slope.astype(BF)
        total = total + dot(act, downs[k][...])
    packed[...] = pack_rows(total[:, :HC], total[:, HC:], 32)


def expert_bwd(slots, slope, *refs):
    ups, downs = refs[:4], refs[4:8]
    flat, d_pre_out, packed = refs[8:]
    low, high = unpack_rows(slots[...], 32)
    rows = jnp.concatenate([low, high], axis=1).astype(BF)
    flat[...] = rows
    total = jnp.zeros((256, C), F32)
    for k in range(4):
        cols = slice(k * 256, (k + 1) * 256)
        d_pre = (slope[:, cols].astype(F32) * dot(rows, downs[k][...], 1, 1)).astype(BF)
        d_pre_out[:, cols] = d_pre
        total = total + dot(d_pre, ups[k][...], 1, 1)
    packed[...] = pack_rows(total[:, :HC], total[:, HC:], 32)


def expert_grads(act, d_rows, rows, d_pre, down_out, up_out):
    down_out[0] = dot(act[...], d_rows[...], 0, 0).astype(BF)
    up_out[0] = dot(rows[...], d_pre[...], 0, 0).astype(BF)


def place_grads(turn, *refs):
    ins, (up_out, down_out) = refs[:8], refs[8:]
    for k in range(4):
        @pl.when(pl.program_id(0) == k)
        def _():
            up_out[0] = ins[k][...].astype(F32)
            down_out[0] = ins[4 + k][...].astype(F32)


def coords():
    s = lax.axis_index("scene")
    row = lax.axis_index("row")
    z, m = row // 4, row % 4
    return s, z, m // 2, m % 2


def at(s, z, y, c):
    return (s, z * 4 + y * 2 + c)


def greet(s, z, y, c):
    barrier = pltpu.get_barrier_semaphore()
    mine = s * 4 + z

    def hail(k, carry):
        peer = (mine + k) % 32
        pl.semaphore_signal(barrier, inc=1, device_id=at(peer // 4, peer % 4, y, c), device_id_type=MESH)
        pl.semaphore_signal(barrier, inc=1, device_id=at(peer // 4, peer % 4, 1 - y, c), device_id_type=MESH)
        return carry

    lax.fori_loop(1, 32, hail, 0)
    pl.semaphore_signal(barrier, inc=1, device_id=at(s, z, 1 - y, c), device_id_type=MESH)
    pl.semaphore_signal(barrier, inc=1, device_id=at(s, z, y, 1 - c), device_id_type=MESH)
    pl.semaphore_wait(barrier, 64)


def dispatch_kernel(src, out, send_sem, recv_sem, pair_send, pair_recv):
    s, z, y, c = coords()
    mine = s * 4 + z
    greet(s, z, y, c)

    def push(k, carry):
        peer = (mine + k) % 32
        for yy in range(2):
            pltpu.make_async_remote_copy(
                src_ref=src.at[peer], dst_ref=out.at[y * 2 + c, mine], send_sem=send_sem, recv_sem=recv_sem.at[y],
                device_id=at(peer // 4, peer % 4, (y + yy) % 2, c), device_id_type=MESH,
            ).start()
        return carry

    pltpu.make_async_copy(src.at[mine], out.at[y * 2 + c, mine], recv_sem.at[y]).start()
    pltpu.make_async_remote_copy(
        src_ref=src.at[mine], dst_ref=out.at[y * 2 + c, mine], send_sem=send_sem, recv_sem=recv_sem.at[y],
        device_id=at(s, z, 1 - y, c), device_id_type=MESH,
    ).start()
    lax.fori_loop(1, 32, push, 0)
    pairs = []
    for yy in range(2):
        block = out.at[yy * 2 + c]
        pltpu.make_async_copy(block, block, recv_sem.at[yy]).wait()
        copy = pltpu.make_async_remote_copy(
            src_ref=block, dst_ref=block, send_sem=pair_send.at[yy], recv_sem=pair_recv.at[yy],
            device_id=at(s, z, y, 1 - c), device_id_type=MESH,
        )
        copy.start()
        pairs.append(copy)
    for copy in pairs:
        copy.wait()
    pltpu.make_async_copy(src, src, send_sem).wait()
    pltpu.make_async_copy(src.at[pl.ds(0, 31)], src.at[pl.ds(0, 31)], send_sem).wait()


def dispatch(slots):
    return pl.pallas_call(
        dispatch_kernel,
        out_shape=sds((4, 32, 16, HC), BF),
        in_specs=[VM],
        out_specs=VM,
        scratch_shapes=[
            pltpu.SemaphoreType.DMA,
            pltpu.SemaphoreType.DMA((2,)),
            pltpu.SemaphoreType.DMA((2,)),
            pltpu.SemaphoreType.DMA((2,)),
        ],
        compiler_params=params(collective_id=0, has_side_effects=True),
        cost_estimate=cost(0, 40 << 20),
        name="dispatch",
    )(slots)


def combine_kernel(part, out, other, total, send_sem, recv_sem, pair_send, pair_recv):
    s, z, y, c = coords()
    mine = s * 4 + z
    greet(s, z, y, c)
    pairs = []
    for yy in range(2):
        copy = pltpu.make_async_remote_copy(
            src_ref=part.at[yy * 2 + (1 - c)], dst_ref=other.at[yy], send_sem=pair_send.at[yy],
            recv_sem=pair_recv.at[yy], device_id=at(s, z, y, 1 - c), device_id_type=MESH,
        )
        copy.start()
        pairs.append(copy)

    def add(yy, peer):
        summed = part[yy * 2 + c, peer].astype(F32) + other[yy, peer].astype(F32)
        total[yy, peer] = summed.astype(BF)

    def ship(yy, peer):
        pltpu.make_async_remote_copy(
            src_ref=total.at[yy, peer], dst_ref=out.at[y, mine], send_sem=send_sem, recv_sem=recv_sem,
            device_id=at(peer // 4, peer % 4, yy, c), device_id_type=MESH,
        ).start()

    for copy in pairs:
        copy.wait_recv()

    def push(k, carry):
        peer = (mine + k) % 32
        add(1 - y, peer)
        ship(1 - y, peer)
        add(y, peer)
        ship(y, peer)
        return carry

    lax.fori_loop(1, 32, push, 0)
    add(1 - y, mine)
    ship(1 - y, mine)
    add(y, mine)
    pltpu.make_async_copy(total.at[y, mine], out.at[y, mine], recv_sem).start()
    for copy in pairs:
        copy.wait_send()
    pltpu.make_async_copy(total, total, recv_sem).wait()
    pltpu.make_async_copy(total.at[0], total.at[0], send_sem).wait()
    pltpu.make_async_copy(total.at[0, pl.ds(0, 31)], total.at[0, pl.ds(0, 31)], send_sem).wait()


def combine(part):
    return pl.pallas_call(
        combine_kernel,
        out_shape=sds((2, 32, 16, HC), BF),
        in_specs=[VM],
        out_specs=VM,
        scratch_shapes=[
            pltpu.VMEM((2, 32, 16, HC), BF),
            pltpu.VMEM((2, 32, 16, HC), BF),
            pltpu.SemaphoreType.DMA,
            pltpu.SemaphoreType.DMA,
            pltpu.SemaphoreType.DMA((2,)),
            pltpu.SemaphoreType.DMA((2,)),
        ],
        compiler_params=params(collective_id=1, has_side_effects=True),
        cost_estimate=cost(0, 40 << 20),
        name="combine",
    )(part)


def row_shift(value, steps):
    pairs = [(source, (source + steps) % 16) for source in range(16)]
    return lax.ppermute(value, "row", pairs)


def z_shift(value, steps):
    pairs = [(z * 4 + m, ((z + steps) % 4) * 4 + m) for z in range(4) for m in range(4)]
    return lax.ppermute(value, "row", pairs)


def bias_pairs():
    spot = np.arange(49)
    py, px = spot // 7, spot % 7
    relative = (py[:, None] - py[None, :] + 6) * 13 + (px[:, None] - px[None, :] + 6)
    table = np.zeros((169, 64, 64), np.float32)
    a, b = np.meshgrid(spot, spot, indexing="ij")
    table[relative.reshape(-1), a.reshape(-1), b.reshape(-1)] = 1.0
    return table.reshape(169, 4096)


def whole(kernel, out_shape, args, specs, scratch=(), flops=0, nbytes=0):
    return pl.pallas_call(
        kernel,
        out_shape=out_shape,
        in_specs=specs,
        out_specs=[VM] * len(out_shape),
        scratch_shapes=list(scratch),
        compiler_params=params(),
        cost_estimate=cost(flops, nbytes),
        name=kernel.__name__,
    )(*args)


def local(
    tokens,
    qkv_weight,
    out_weight,
    position_bias,
    window_shift,
    expert_up,
    expert_down,
    expert_choice,
    combine_weight,
    reduce_weight,
    merged_grad,
):
    row = lax.axis_index("row")
    z = row // 4
    x = jnp.pad(tokens.reshape(TOK, C), ((0, TP - TOK), (0, 0)))
    scal = jnp.stack([window_shift[0], window_shift[1], (row == 15).astype(jnp.int32), z.astype(jnp.int32)])
    choice = jnp.pad(expert_choice.reshape(TOK), (0, TP - TOK), constant_values=-1000)
    gate = jnp.pad(combine_weight.reshape(TOK, 1), ((0, TP - TOK), (0, 0)))

    below = row_shift(x[:HALO], -1)
    ups, downs = [], []
    for k in range(4):
        expert = (z + k) % 4
        up_k = lax.dynamic_index_in_dim(expert_up, expert, 0, keepdims=False)
        down_k = lax.dynamic_index_in_dim(expert_down, expert, 0, keepdims=False)
        ups.append(z_shift(up_k, k) if k else up_k)
        downs.append(z_shift(down_k, k) if k else down_k)

    d_parts = jnp.einsum(
        "nkd,cd->nkc", merged_grad.reshape(8, 49, -1), reduce_weight, preferred_element_type=F32
    ).astype(BF)
    d_parts = lax.all_to_all(d_parts, "scene", split_axis=0, concat_axis=0, tiled=True)

    bias = jnp.dot(position_bias, jnp.asarray(bias_pairs()), precision=lax.Precision.HIGHEST).reshape(32, 64, 64)

    full = lambda shape: pl.BlockSpec(shape, lambda g: (0,) * len(shape))
    w_spec = lambda which: pl.BlockSpec((C, GRP), lambda g: (0, 4 * which + g))
    wo_spec = pl.BlockSpec((GRP, C), lambda g: (g, 0))
    head_spec = pl.BlockSpec((TP, GRP), lambda g: (0, g))
    prob_spec = pl.BlockSpec((8 * TP, TP), lambda g: (g, 0))
    att, q, k, v, probs = pl.pallas_call(
        attn_fwd,
        grid=(4,),
        out_shape=[sds((TP, C), BF)] * 4 + [sds((32 * TP, TP), BF)],
        in_specs=[SM, full((TP, C)), full((HALO, C)), w_spec(0), w_spec(1), w_spec(2), wo_spec,
                  pl.BlockSpec((8, 64, 64), lambda g: (g, 0, 0))],
        out_specs=[full((TP, C)), head_spec, head_spec, head_spec, prob_spec],
        scratch_shapes=[pltpu.VMEM((TP, C), BF), pltpu.VMEM((TP, TP), F32), pltpu.VMEM((192, TP), BF),
                        pltpu.VMEM((TP, 192), BF), pltpu.VMEM((TP, C), F32)],
        compiler_params=params(),
        cost_estimate=cost(6 << 30, 14 << 20),
        name="attn_fwd",
    )(scal, x, below, qkv_weight, qkv_weight, qkv_weight, out_weight, bias)

    above = row_shift(att[:HALO], 1)
    after, slots, table = whole(
        route,
        [sds((TP, C), BF), sds((32, 16, HC), BF), sds((TP, 256), BF)],
        (scal, x, att, above, choice.reshape(TP, 1), choice.reshape(1, TP)),
        [SM] + [VM] * 5, flops=1 << 30, nbytes=4 << 20,
    )
    slot_in = dispatch(slots).reshape(128, 16, HC)

    slot_spec = pl.BlockSpec((32, 16, HC), lambda g: (g, 0, 0))
    row_spec = pl.BlockSpec((256, C), lambda g: (g, 0))
    weight_specs = [full((C, 256))] * 4 + [full((256, C))] * 4
    flat_in, act, slope, part = pl.pallas_call(
        expert_fwd,
        grid=(4,),
        out_shape=[sds((C, C), BF)] * 3 + [sds((128, 16, HC), BF)],
        in_specs=[slot_spec] + weight_specs,
        out_specs=[row_spec] * 3 + [slot_spec],
        compiler_params=params(),
        cost_estimate=cost(4 << 30, 14 << 20),
        name="expert_fwd",
    )(slot_in, *ups, *downs)
    ret = combine(part.reshape(4, 32, 16, HC))

    merge_norm, d_block, d_slots = whole(
        merge_mid,
        [sds((49, 4 * C), BF), sds((TP, C), F32), sds((32, 16, HC), BF)],
        (after, ret, table, gate, d_parts),
        [VM] * 5, scratch=[pltpu.VMEM((256, C), F32)], flops=2 << 30, nbytes=8 << 20,
    )
    d_slot_in = dispatch(d_slots).reshape(128, 16, HC)
    flat_d, d_pre, d_part = pl.pallas_call(
        expert_bwd,
        grid=(4,),
        out_shape=[sds((C, C), BF)] * 2 + [sds((128, 16, HC), BF)],
        in_specs=[slot_spec, row_spec] + weight_specs,
        out_specs=[row_spec] * 2 + [slot_spec],
        compiler_params=params(),
        cost_estimate=cost(4 << 30, 14 << 20),
        name="expert_bwd",
    )(d_slot_in, slope, *ups, *downs)
    d_ret = combine(d_part.reshape(4, 32, 16, HC))

    col_spec = pl.BlockSpec((C, 256), lambda g: (0, g))
    down_parts, up_parts = pl.pallas_call(
        expert_grads,
        grid=(4,),
        out_shape=[sds((4, 256, C), BF), sds((4, C, 256), BF)],
        in_specs=[col_spec, full((C, C)), full((C, C)), col_spec],
        out_specs=[pl.BlockSpec((1, 256, C), lambda g: (g, 0, 0)), pl.BlockSpec((1, C, 256), lambda g: (g, 0, 0))],
        compiler_params=params(),
        cost_estimate=cost(4 << 30, 14 << 20),
        name="expert_grads",
    )(act, flat_d, flat_in, d_pre)
    up_back = [up_parts[0]] + [z_shift(up_parts[k], -k) for k in range(1, 4)]
    down_back = [down_parts[0]] + [z_shift(down_parts[k], -k) for k in range(1, 4)]

    d_after, d_att = whole(
        after_back, [sds((TP, C), F32), sds((TP, C), BF)], (after, d_ret, table, d_block), [VM] * 4,
        flops=1 << 30, nbytes=4 << 20,
    )
    d_below = row_shift(d_att[:HALO], -1)
    d_shift = pl.pallas_call(
        attn_bwd,
        grid=(4,),
        out_shape=sds((TP, C), BF),
        in_specs=[SM, full((TP, C)), full((HALO, C)), w_spec(0), w_spec(1), w_spec(2), wo_spec,
                  head_spec, head_spec, head_spec, prob_spec],
        out_specs=full((TP, C)),
        scratch_shapes=[pltpu.VMEM((TP, C), BF), pltpu.VMEM((TP, C), F32)],
        compiler_params=params(),
        cost_estimate=cost(8 << 30, 14 << 20),
        name="attn_bwd",
    )(scal, d_att, d_below, qkv_weight, qkv_weight, qkv_weight, out_weight, q, k, v, probs)
    d_above = row_shift(d_shift[:HALO], 1)
    (grad,) = whole(
        finish, [sds((TP, C), BF)], (scal, x, d_after, d_shift, d_above), [SM] + [VM] * 4,
        flops=1 << 28, nbytes=3 << 20,
    )
    tokens_grad = grad[:TOK].reshape(tokens.shape)

    merged = jnp.einsum(
        "nkc,cd->nkd", lax.all_gather(merge_norm[None], "scene", axis=0, tiled=True), reduce_weight,
        preferred_element_type=F32,
    ).astype(BF).reshape(merged_grad.shape)

    up_grad, down_grad = pl.pallas_call(
        place_grads,
        grid_spec=pltpu.PrefetchScalarGridSpec(
            num_scalar_prefetch=1,
            grid=(4,),
            in_specs=[pl.BlockSpec((C, 256), lambda g, t: (0, 0))] * 4 + [pl.BlockSpec((256, C), lambda g, t: (0, 0))] * 4,
            out_specs=[pl.BlockSpec((1, C, 256), lambda g, t: ((t[0] + g) % 4, 0, 0)),
                       pl.BlockSpec((1, 256, C), lambda g, t: ((t[0] + g) % 4, 0, 0))],
        ),
        out_shape=[sds((4, C, 256), F32), sds((4, 256, C), F32)],
        compiler_params=params(),
        cost_estimate=cost(0, 12 << 20),
        name="place_grads",
    )(z.reshape(1).astype(jnp.int32), *up_back, *down_back)
    return (merged, tokens_grad, up_grad, down_grad)


def solution(mesh):
    placed = (
        P("scene", "row", None, None),
        P(),
        P(),
        P(),
        P(),
        P("scene", None, "row"),
        P("scene", "row", None),
        P("scene", "row", None, None),
        P("scene", "row", None),
        P(None, "scene"),
        P(None, "row", None, "scene"),
    )
    return jax.shard_map(
        local,
        mesh=mesh,
        in_specs=placed,
        out_specs=(
            P(None, "row", None, "scene"),
            P("scene", "row", None, None),
            P("scene", None, "row"),
            P("scene", "row", None),
        ),
        check_vma=False,
    )
```

time: 859 us -> 363 us (0.42)
  waiting for transfers between devices: 496 us -> 40 us
  Pallas kernels: 0 us -> 241 us
  local copies, waits for them, and re-layouts: 120 us -> 20.7 us
  matrix products: 101 us -> 9.09 us
  other arithmetic: 62 us -> 1.37 us
  blocking collectives: 29.3 us -> 0 us
  starting transfers between devices: 21 us -> 30.4 us
    unnamed x8 -> x1, waiting for transfers between devices: 390 us -> 0.02 us
    pallas_call x0 -> x14, Pallas kernels: none -> 241 us  [the longest x2 81.1 us: dispatch(): pl.pallas_call(dispatch_kernel, out_shape=sds((4, 32, 16, HC), BF), in_sp...]
    all_gather x3 -> x1, waiting for transfers between devices: 86.7 us -> 0.01 us  [local(): lax.all_gather(merge_norm[None], 'scene', axis=0, tiled=True)]
    dot_general x22 -> x3, matrix products: 95.6 us -> 9.09 us  [the longest x1 3.92 us: local(): jnp.einsum('nkd,cd->nkc', merged_grad.reshape(8, 49, -1), reduce_weight,...]
    reshape x23 -> x6, local copies, waits for them, and re-layouts: 36.3 us -> 3.34 us  [the longest x1 1.38 us: local(): jnp.dot(position_bias, jnp.asarray(bias_pairs()), precision=lax.Precision...]
    ppermute x4 -> x16, waiting for transfers between devices: 8.74 us -> 40 us  [the longest x4 24.1 us: row_shift(): return lax.ppermute(value, 'row', pairs)]
    reduce_sum x12 -> x0, other arithmetic: 30.4 us -> none  [the longest x3 9.29 us: layer_norm(): centred = values - centre]
    all_to_all x2 -> x0, blocking collectives: 29.3 us -> none  [to_owner(): lax.all_to_all(grouped, 'scene', split_axis=0, concat_axis=0, tiled=True)]
  transfers between devices with their start and end apart: 12 -> 18, of which waited for: 7 -> 3; matrix products, arithmetic and copies ran while one was open for 9% -> 6% of each run, Pallas kernels for 0% -> 66%
where the time goes in v1:
time: 363 us; the launch traced here: 357 us
  Pallas kernels  241 us (66%)
  waiting for transfers between devices  40 us (11%)
  starting transfers between devices  30.4 us (8%)
  local copies, waits for them, and re-layouts  20.7 us (6%)
  between operations  14.3 us (4%)
  matrix products  9.09 us (3%)
    pallas_call x2, Pallas kernels, dispatch(): pl.pallas_call(dispatch_kernel, out_shape=sds((4, 32, 16, HC), BF), in_sp...  81.1 us
    pallas_call x2, Pallas kernels, combine(): pl.pallas_call(combine_kernel, out_shape=sds((2, 32, 16, HC), BF), in_spe...  69.5 us
    ppermute x4, waiting for transfers between devices, row_shift(): return lax.ppermute(value, 'row', pairs)  24.1 us
    pallas_call x1, Pallas kernels, local(): pl.pallas_call(attn_fwd, grid=(4,), out_shape=[sds((TP, C), BF)] * 4 + [s...  19.7 us
    pallas_call x1, Pallas kernels, local(): pl.pallas_call(attn_bwd, grid=(4,), out_shape=sds((TP, C), BF), in_specs=...  19.5 us
    ppermute x12, starting transfers between devices, z_shift(): return lax.ppermute(value, 'row', pairs)  16.2 us
    ppermute x12, waiting for transfers between devices, z_shift(): return lax.ppermute(value, 'row', pairs)  15.9 us
    pallas_call x4, Pallas kernels, whole(): pl.pallas_call(kernel, out_shape=out_shape, in_specs=specs, out_specs=[VM...  14.6 us
  transfers between devices with their start and end apart: 18, of which 3 were waited for; matrix products, arithmetic and copies ran while one was open for 6% of the time, Pallas kernels for 66%

profile of v1, /device:TPU:0, one launch (start us, length us, event | category | flops | bytes accessed | tf_op | source)
XLA Modules:
  0.0 357.2 jit_solution(945043596027499596)
XLA Ops:
  8.8 3.9 %convolution_convert_fusion = bf16[8,49,4096]{2,1,0:T(8,128)(2,1)} fusion(bf16[4096,256]{1,0:T(8,128)(2,1)S(1)} %copy-done, bf16[8,49,256]{2,0,1:T(8,128)(2,1)} %bitcast.60), kind=kOutput, calls=%fused_computation | convolution fusion | flops 823689216 | bytes 5509120 | tf_op jit(solution)/shard_map/nkd,cd->nkc/dot_general | solution.py:531
  12.7 7.1 %all-to-all-start = ((bf16[8,49,4096]{2,1,0:T(8,128)(2,1)}), bf16[8,49,4096]{2,1,0:T(8,128)(2,1)}, u32[]{:S(2)}, u32[]{:S(2)}) async-start(bf16[8,49,4096]{2,1,0:T(8,128)(2,1)} %convolution_convert_fusion), calls=%async_computation | async-start | bytes 7340032 | tf_op jit(solution)/shard_map/all_to_all | solution.py:534
  20.7 3.3 collective-permute-start
  24.0 2.8 dynamic-slice_bitcast_fusion.4
  33.1 18.6 %collective-permute-done.halo = bf16[96,1024]{1,0:T(8,128)(2,1)} collective-permute-done((bf16[96,1024]{1,0:T(8,128)(2,1)}, bf16[96,1024]{1,0:T(8,128)(2,1)}, u32[]{:S(2)}, u32[]{:S(2)}) %collective-permute-start) | collective-permute-done | bytes 196640 | tf_op jit(solution)/shard_map/ppermute | solution.py:471
  51.7 19.7 %attn_fwd.1 = (bf16[208,1024]{1,0:T(8,128)(2,1)}, bf16[208,1024]{1,0:T(8,128)(2,1)}, bf16[208,1024]{1,0:T(8,128)(2,1)}, bf16[208,1024]{1,0:T(8,128)(2,1)}, bf16[6656,208]{1,0:T(8,128)(2,1)}) custom-call(s32[4]{0:T(128)} %pad_add_fusion.scal, bf16[208,1024]{1,0:T(8,128)(2,1)} %pad.12.x, bf16[96,1024]{1,0:T(8,128)(2,1)} %collective-permute-done.halo, ...), custom_call_target="tpu_custom_call" | custom-call | flops 6442450944 | bytes 14680064 | tf_op jit(solution)/shard_map/attn_fwd/pallas_call | solution.py:543
  75.7 3.6 %collective-permute-start.3 = (bf16[1024,256]{1,0:T(8,128)(2,1)S(1)}, bf16[1024,256]{1,0:T(8,128)(2,1)}, u32[]{:S(2)}, u32[]{:S(2)}) collective-permute-start(bf16[1024,256]{1,0:T(8,128)(2,1)S(1)} %get-tuple-element.71), channel_id=1, source_target_pairs={{0,8},{1,9},{2,10},{3,11},{4,12},{5,13},{6,14},{7,15},{8,0},{9,1},... | collective-permute-start | bytes 1572872 | tf_op jit(solution)/shard_map/ppermute | solution.py:476
  86.2 2.8 route.1
  89.0 52.9 %dispatch.2 = bf16[4,32,16,512]{3,2,1,0:T(8,128)(2,1)} custom-call(bf16[32,16,512]{2,1,0:T(8,128)(2,1)} %get-tuple-element.30.src), custom_call_target="tpu_custom_call" | custom-call | bytes 41943040 | tf_op jit(solution)/shard_map/dispatch/pallas_call | solution.py:386
  142.0 11.6 %expert_fwd.1 = (bf16[1024,1024]{1,0:T(8,128)(2,1)}, bf16[1024,1024]{1,0:T(8,128)(2,1)}, bf16[1024,1024]{1,0:T(8,128)(2,1)}, bf16[128,16,512]{2,1,0:T(8,128)(2,1)}) custom-call(bf16[128,16,512]{2,1,0:T(8,128)(2,1)} %bitcast.55, bf16[1024,256]{1,0:T(8,128)(2,1)} %get-tuple-element.70.refs_0_, bf16[1024,256]{1,0:T(8,128)(2,1)} %collective-permute-done.2.refs_1_, ...), custom_call_target="tpu_custom_call" | custom-call | flops 4294967296 | bytes 14680064 | tf_op jit(solution)/shard_map/expert_fwd/pallas_call | solution.py:569
  153.7 38.3 %combine.2.ret = bf16[2,32,16,512]{3,2,1,0:T(8,128)(2,1)} custom-call(bf16[4,32,16,512]{3,2,1,0:T(8,128)(2,1)} %bitcast.58), custom_call_target="tpu_custom_call" | custom-call | bytes 41943040 | tf_op jit(solution)/shard_map/combine/pallas_call | solution.py:450
  191.9 5.7 %merge_mid.1 = (bf16[49,4096]{1,0:T(8,128)(2,1)}, f32[208,1024]{1,0:T(8,128)}, bf16[32,16,512]{2,1,0:T(8,128)(2,1)}) custom-call(bf16[208,1024]{1,0:T(8,128)(2,1)} %get-tuple-element.29.after, bf16[2,32,16,512]{3,2,1,0:T(8,128)(2,1)} %combine.2.ret, bf16[208,256]{1,0:T(8,128)(2,1)} %get-tuple-element.32.table_in.table, f32[208,1]{1,0:T(8,128)} %pad.14.gate_in, ...), custom_call_target="tpu_custom_call" | custom-call | flops 2147483648 | bytes 8388608 | tf_op jit(solution)/shard_map/merge_mid/pallas_call | solution.py:490
  197.6 28.2 %dispatch.3 = bf16[4,32,16,512]{3,2,1,0:T(8,128)(2,1)} custom-call(bf16[32,16,512]{2,1,0:T(8,128)(2,1)} %get-tuple-element.34.src), custom_call_target="tpu_custom_call" | custom-call | bytes 41943040 | tf_op jit(solution)/shard_map/dispatch/pallas_call | solution.py:386
  225.8 10.7 %expert_bwd.1 = (bf16[1024,1024]{1,0:T(8,128)(2,1)}, bf16[1024,1024]{1,0:T(8,128)(2,1)}, bf16[128,16,512]{2,1,0:T(8,128)(2,1)}) custom-call(bf16[128,16,512]{2,1,0:T(8,128)(2,1)} %bitcast.56, bf16[1024,1024]{1,0:T(8,128)(2,1)} %get-tuple-element.35.slope, bf16[1024,256]{1,0:T(8,128)(2,1)} %get-tuple-element.70.refs_0_, ...), custom_call_target="tpu_custom_call" | custom-call | flops 4294967296 | bytes 14680064 | tf_op jit(solution)/shard_map/expert_bwd/pallas_call | solution.py:588
  236.5 31.3 %combine.3.ret = bf16[2,32,16,512]{3,2,1,0:T(8,128)(2,1)} custom-call(bf16[4,32,16,512]{3,2,1,0:T(8,128)(2,1)} %bitcast.57), custom_call_target="tpu_custom_call" | custom-call | bytes 41943040 | tf_op jit(solution)/shard_map/combine/pallas_call | solution.py:450
  267.8 3.4 after_back.1
  274.4 8.7 %expert_grads.1 = (bf16[4,256,1024]{2,1,0:T(8,128)(2,1)}, bf16[4,1024,256]{2,1,0:T(8,128)(2,1)}) custom-call(bf16[1024,1024]{1,0:T(8,128)(2,1)} %get-tuple-element.44.act, bf16[1024,1024]{1,0:T(8,128)(2,1)} %get-tuple-element.45.d_rows, bf16[1024,1024]{1,0:T(8,128)(2,1)} %get-tuple-element.46.rows, bf16[1024,1024]{1,0:T(8,128)(2,1)} %get-tuple-element.47.d_pre), custom_call_target="tpu_custom_call" | custom-call | flops 4294967296 | bytes 14680064 | tf_op jit(solution)/shard_map/expert_grads/pallas_call | solution.py:601
  283.1 2.7 slice_bitcast_fusion.4
  290.4 19.5 %attn_bwd.1.own = bf16[208,1024]{1,0:T(8,128)(2,1)} custom-call(s32[4]{0:T(128)} %pad_add_fusion.scal, bf16[208,1024]{1,0:T(8,128)(2,1)} %get-tuple-element.39.own, bf16[96,1024]{1,0:T(8,128)(2,1)} %copy-done.14, bf16[1024,3072]{1,0:T(8,128)(2,1)} %wv.3, bf16[1024,3072]{1,0:T(8,128)(2,1)} %wv.3, bf16[1024,3072]{1,0:T(8,128)(2,1)} %wv.3, ...), custom_call_target="tpu_custom_call" | custom-call | flops 8589934592 | bytes 14680064 | tf_op jit(solution)/shard_map/attn_bwd/pallas_call | solution.py:619
  312.7 5.5 %collective-permute-done.9.halo = bf16[96,1024]{1,0:T(8,128)(2,1)S(1)} collective-permute-done((bf16[96,1024]{1,0:T(8,128)(2,1)S(1)}, bf16[96,1024]{1,0:T(8,128)(2,1)S(1)}, u32[]{:S(2)}, u32[]{:S(2)}) %collective-permute-start.9) | collective-permute-done | bytes 196640 | tf_op jit(solution)/shard_map/ppermute | solution.py:471
  320.1 2.8 finish.1
  324.8 15.9 %collective-permute-done.15.refs_7_ = bf16[256,1024]{1,0:T(8,128)(2,1)} collective-permute-done((bf16[256,1024]{1,0:T(8,128)(2,1)}, bf16[256,1024]{1,0:T(8,128)(2,1)}, u32[]{:S(2)}, u32[]{:S(2)}) %collective-permute-start.15) | collective-permute-done | bytes 524320 | tf_op jit(solution)/shard_map/ppermute | solution.py:476
  340.7 5.8 %place_grads.1 = (f32[4,1024,256]{2,1,0:T(8,128)}, f32[4,256,1024]{2,1,0:T(8,128)}) custom-call(s32[1]{0:T(128)} %bitcast.1.turn, bf16[1024,256]{1,0:T(8,128)(2,1)} %get-tuple-element.63.refs_0_, bf16[1024,256]{1,0:T(8,128)(2,1)} %collective-permute-done.10.refs_1_, bf16[1024,256]{1,0:T(8,128)(2,1)} %copy-done.5, bf16[1024,256]{1,0:T(8,128)(2,1)} %copy-done.4, ...), custom_call_target="tpu_custom_call" | custom-call | bytes 12582912 | tf_op jit(solution)/shard_map/place_grads/pallas_call | solution.py:643
  346.5 3.2 fusion.3
  (82 shorter events, 34.9 us)
Async XLA Ops:
  12.7 179.2 %all-to-all-start = ((bf16[8,49,4096]{2,1,0:T(8,128)(2,1)}), bf16[8,49,4096]{2,1,0:T(8,128)(2,1)}, u32[]{:S(2)}, u32[]{:S(2)}) async-start(bf16[8,49,4096]{2,1,0:T(8,128)(2,1)} %convolution_convert_fusion), calls=%async_computation | async-start | bytes 7340032 | tf_op jit(solution)/shard_map/all_to_all | solution.py:534
  19.8 326.6 %all-gather.4.cloned.1.call-start = ((), (), s32[]{:S(2)}) async-start(), calls=%async_computation.1 | async-start | bytes 4128768 | tf_op jit(solution)/shard_map/all_gather | solution.py:639
  20.7 31.0 %collective-permute-start = (bf16[96,1024]{1,0:T(8,128)(2,1)}, bf16[96,1024]{1,0:T(8,128)(2,1)}, u32[]{:S(2)}, u32[]{:S(2)}) collective-permute-start(bf16[96,1024]{1,0:T(8,128)(2,1)} %slice.56), channel_id=1, source_target_pairs={{0,15},{1,0},{2,1},{3,2},{4,3},{5,4},{6,5},{7,6},{8,7},{9,8},{10,9... | collective-permute-start | bytes 589832 | tf_op jit(solution)/shard_map/ppermute | solution.py:471
  26.9 55.9 %collective-permute-start.4 = (bf16[1024,256]{1,0:T(8,128)(2,1)}, bf16[1024,256]{1,0:T(8,128)(2,1)}, u32[]{:S(2)}, u32[]{:S(2)}) collective-permute-start(bf16[1024,256]{1,0:T(8,128)(2,1)} %get-tuple-element.68), channel_id=1, source_target_pairs={{0,12},{1,13},{2,14},{3,15},{4,0},{5,1},{6,2},{7,3},{8,4},{9,5},{1... | collective-permute-start | bytes 1572872 | tf_op jit(solution)/shard_map/ppermute | solution.py:476
  33.1 40.7 %copy-start.6 = (bf16[1024,256]{1,0:T(8,128)(2,1)S(1)}, bf16[1024,256]{1,0:T(8,128)(2,1)}, u32[]{:S(2)}) copy-start(bf16[1024,256]{1,0:T(8,128)(2,1)} %get-tuple-element.69) | copy-start | bytes 1572868
  33.1 46.2 %copy-start.3 = (bf16[4,256,1024]{2,1,0:T(8,128)(2,1)S(1)}, bf16[4,256,1024]{2,1,0:T(8,128)(2,1)}, u32[]{:S(2)}) copy-start(bf16[4,256,1024]{2,1,0:T(8,128)(2,1)} %param.18) | copy-start | bytes 6291460
  72.4 9.3 %collective-permute-start.1 = (bf16[96,1024]{1,0:T(8,128)(2,1)S(1)}, bf16[96,1024]{1,0:T(8,128)(2,1)S(1)}, u32[]{:S(2)}, u32[]{:S(2)}) collective-permute-start(bf16[96,1024]{1,0:T(8,128)(2,1)S(1)} %slice.44), channel_id=1, source_target_pairs={{0,1},{1,2},{2,3},{3,4},{4,5},{5,6},{6,7},{7,8},{8,9},{9,10},{10,1... | collective-permute-start | bytes 589832 | tf_op jit(solution)/shard_map/ppermute | solution.py:471
  73.8 68.2 %collective-permute-start.2 = (bf16[1024,256]{1,0:T(8,128)(2,1)S(1)}, bf16[1024,256]{1,0:T(8,128)(2,1)}, u32[]{:S(2)}, u32[]{:S(2)}) collective-permute-start(bf16[1024,256]{1,0:T(8,128)(2,1)S(1)} %copy-done.6), channel_id=1, source_target_pairs={{0,4},{1,5},{2,6},{3,7},{4,8},{5,9},{6,10},{7,11},{8,12},{9,13},{1... | collective-permute-start | bytes 1572872 | tf_op jit(solution)/shard_map/ppermute | solution.py:476
  75.7 8.9 %copy-start.11 = (f32[1,14,14]{2,0,1:T(1,128)S(1)}, f32[1,14,14]{2,0,1:T(1,128)}, u32[]{:S(2)}) copy-start(f32[1,14,14]{2,0,1:T(1,128)} %param.20) | copy-start | bytes 2356
  75.7 66.3 %collective-permute-start.3 = (bf16[1024,256]{1,0:T(8,128)(2,1)S(1)}, bf16[1024,256]{1,0:T(8,128)(2,1)}, u32[]{:S(2)}, u32[]{:S(2)}) collective-permute-start(bf16[1024,256]{1,0:T(8,128)(2,1)S(1)} %get-tuple-element.71), channel_id=1, source_target_pairs={{0,8},{1,9},{2,10},{3,11},{4,12},{5,13},{6,14},{7,15},{8,0},{9,1},... | collective-permute-start | bytes 1572872 | tf_op jit(solution)/shard_map/ppermute | solution.py:476
  80.7 61.3 %collective-permute-start.7 = (bf16[256,1024]{1,0:T(8,128)(2,1)}, bf16[256,1024]{1,0:T(8,128)(2,1)}, u32[]{:S(2)}, u32[]{:S(2)}) collective-permute-start(bf16[256,1024]{1,0:T(8,128)(2,1)} %get-tuple-element.64), channel_id=1, source_target_pairs={{0,12},{1,13},{2,14},{3,15},{4,0},{5,1},{6,2},{7,3},{8,4},{9,5},{1... | collective-permute-start | bytes 1572872 | tf_op jit(solution)/shard_map/ppermute | solution.py:476
  81.7 60.3 %collective-permute-start.5 = (bf16[256,1024]{1,0:T(8,128)(2,1)}, bf16[256,1024]{1,0:T(8,128)(2,1)}, u32[]{:S(2)}, u32[]{:S(2)}) collective-permute-start(bf16[256,1024]{1,0:T(8,128)(2,1)} %get-tuple-element.65), channel_id=1, source_target_pairs={{0,4},{1,5},{2,6},{3,7},{4,8},{5,9},{6,10},{7,11},{8,12},{9,13},{1... | collective-permute-start | bytes 1572872 | tf_op jit(solution)/shard_map/ppermute | solution.py:476
  82.7 59.3 %collective-permute-start.6 = (bf16[256,1024]{1,0:T(8,128)(2,1)}, bf16[256,1024]{1,0:T(8,128)(2,1)}, u32[]{:S(2)}, u32[]{:S(2)}) collective-permute-start(bf16[256,1024]{1,0:T(8,128)(2,1)} %get-tuple-element.67), channel_id=1, source_target_pairs={{0,8},{1,9},{2,10},{3,11},{4,12},{5,13},{6,14},{7,15},{8,0},{9,1},... | collective-permute-start | bytes 1572872 | tf_op jit(solution)/shard_map/ppermute | solution.py:476
  272.1 17.6 %collective-permute-start.8 = (bf16[96,1024]{1,0:T(8,128)(2,1)S(1)}, bf16[96,1024]{1,0:T(8,128)(2,1)S(1)}, u32[]{:S(2)}, u32[]{:S(2)}) collective-permute-start(bf16[96,1024]{1,0:T(8,128)(2,1)S(1)} %slice.45), channel_id=1, source_target_pairs={{0,15},{1,0},{2,1},{3,2},{4,3},{5,4},{6,5},{7,6},{8,7},{9,8},{10,9... | collective-permute-start | bytes 589832 | tf_op jit(solution)/shard_map/ppermute | solution.py:471
  285.8 33.4 %collective-permute-start.12 = (bf16[1024,256]{1,0:T(8,128)(2,1)S(1)}, bf16[1024,256]{1,0:T(8,128)(2,1)S(1)}, u32[]{:S(2)}, u32[]{:S(2)}) collective-permute-start(bf16[1024,256]{1,0:T(8,128)(2,1)S(1)} %get-tuple-element.60), channel_id=1, source_target_pairs={{0,4},{1,5},{2,6},{3,7},{4,8},{5,9},{6,10},{7,11},{8,12},{9,13},{1... | collective-permute-start | bytes 1572872 | tf_op jit(solution)/shard_map/ppermute | solution.py:476
  285.8 38.9 %collective-permute-start.11 = (bf16[1024,256]{1,0:T(8,128)(2,1)}, bf16[1024,256]{1,0:T(8,128)(2,1)S(1)}, u32[]{:S(2)}, u32[]{:S(2)}) collective-permute-start(bf16[1024,256]{1,0:T(8,128)(2,1)} %get-tuple-element.61), channel_id=1, source_target_pairs={{0,8},{1,9},{2,10},{3,11},{4,12},{5,13},{6,14},{7,15},{8,0},{9,1},... | collective-permute-start | bytes 1572872 | tf_op jit(solution)/shard_map/ppermute | solution.py:476
  288.1 36.7 %collective-permute-start.10 = (bf16[1024,256]{1,0:T(8,128)(2,1)}, bf16[1024,256]{1,0:T(8,128)(2,1)}, u32[]{:S(2)}, u32[]{:S(2)}) collective-permute-start(bf16[1024,256]{1,0:T(8,128)(2,1)} %get-tuple-element.62), channel_id=1, source_target_pairs={{0,12},{1,13},{2,14},{3,15},{4,0},{5,1},{6,2},{7,3},{8,4},{9,5},{1... | collective-permute-start | bytes 1572872 | tf_op jit(solution)/shard_map/ppermute | solution.py:476
  290.4 20.5 %copy-start.2 = (bf16[4,256,1024]{2,1,0:T(8,128)(2,1)S(1)}, bf16[4,256,1024]{2,1,0:T(8,128)(2,1)}, u32[]{:S(2)}) copy-start(bf16[4,256,1024]{2,1,0:T(8,128)(2,1)} %get-tuple-element.49) | copy-start | bytes 6291460
  310.8 7.4 %collective-permute-start.9 = (bf16[96,1024]{1,0:T(8,128)(2,1)S(1)}, bf16[96,1024]{1,0:T(8,128)(2,1)S(1)}, u32[]{:S(2)}, u32[]{:S(2)}) collective-permute-start(bf16[96,1024]{1,0:T(8,128)(2,1)S(1)} %slice.57), channel_id=1, source_target_pairs={{0,1},{1,2},{2,3},{3,4},{4,5},{5,6},{6,7},{7,8},{8,9},{9,10},{10,1... | collective-permute-start | bytes 589832 | tf_op jit(solution)/shard_map/ppermute | solution.py:471
  312.2 28.4 %collective-permute-start.15 = (bf16[256,1024]{1,0:T(8,128)(2,1)}, bf16[256,1024]{1,0:T(8,128)(2,1)}, u32[]{:S(2)}, u32[]{:S(2)}) collective-permute-start(bf16[256,1024]{1,0:T(8,128)(2,1)} %get-tuple-element.56), channel_id=1, source_target_pairs={{0,4},{1,5},{2,6},{3,7},{4,8},{5,9},{6,10},{7,11},{8,12},{9,13},{1... | collective-permute-start | bytes 1572872 | tf_op jit(solution)/shard_map/ppermute | solution.py:476
  318.2 22.5 %collective-permute-start.14 = (bf16[256,1024]{1,0:T(8,128)(2,1)}, bf16[256,1024]{1,0:T(8,128)(2,1)}, u32[]{:S(2)}, u32[]{:S(2)}) collective-permute-start(bf16[256,1024]{1,0:T(8,128)(2,1)} %get-tuple-element.57), channel_id=1, source_target_pairs={{0,8},{1,9},{2,10},{3,11},{4,12},{5,13},{6,14},{7,15},{8,0},{9,1},... | collective-permute-start | bytes 1572872 | tf_op jit(solution)/shard_map/ppermute | solution.py:476
  319.3 21.4 %copy-start.4 = (bf16[1024,256]{1,0:T(8,128)(2,1)}, bf16[1024,256]{1,0:T(8,128)(2,1)S(1)}, u32[]{:S(2)}) copy-start(bf16[1024,256]{1,0:T(8,128)(2,1)S(1)} %collective-permute-done.12.refs_3_) | copy-start | bytes 1572868
  319.3 21.4 %collective-permute-start.13 = (bf16[256,1024]{1,0:T(8,128)(2,1)}, bf16[256,1024]{1,0:T(8,128)(2,1)}, u32[]{:S(2)}, u32[]{:S(2)}) collective-permute-start(bf16[256,1024]{1,0:T(8,128)(2,1)} %get-tuple-element.58), channel_id=1, source_target_pairs={{0,12},{1,13},{2,14},{3,15},{4,0},{5,1},{6,2},{7,3},{8,4},{9,5},{1... | collective-permute-start | bytes 1572872 | tf_op jit(solution)/shard_map/ppermute | solution.py:476
  324.8 15.9 %copy-start.5 = (bf16[1024,256]{1,0:T(8,128)(2,1)}, bf16[1024,256]{1,0:T(8,128)(2,1)S(1)}, u32[]{:S(2)}) copy-start(bf16[1024,256]{1,0:T(8,128)(2,1)S(1)} %collective-permute-done.11.refs_2_) | copy-start | bytes 1572868
  (9 other events, 33.2 us)
Sparse Core Ops, SparseCore 0:
  197.8 89.3 all-gather.3

commit v2 on v1

--- a/solution.py
+++ b/solution.py
@@ -103,36 +103,31 @@
     return low, high
 
 
-def attn_fwd(scal, x, halo, wq, wk, wv, wo, bias, att, q_out, k_out, v_out, p_out, normed, mask, ecol, erow, acc):
-    g = pl.program_id(0)
-
-    @pl.when(g == 0)
-    def _():
-        r, c, last = scal[0], scal[1], scal[2]
-        own = x[:HALO, :].astype(F32)
-        top = jnp.where(iota((HALO, C), 0) < 14 * r, halo[...].astype(F32), own)
-        normed[:HALO, :] = norm_parts(top)[0].astype(BF)
-        normed[HALO:, :] = norm_parts(x[HALO:, :].astype(F32))[0].astype(BF)
-        tq, tk = iota((TP, TP), 0), iota((TP, TP), 1)
-        wq_, lq = group_of(tq, r, c, last)
-        wk_, lk = group_of(tk, r, c, last)
-        open_ = jnp.where(lq == lk, 0.0, -100.0)
-        seen = jnp.where(wq_ == wk_, open_, NEG)
-        mask[...] = jnp.where(tk < TOK, seen, NEG)
-        row_pos = pos_of(iota((TP, 192), 0), r, c)
-        erow[...] = jnp.where(row_pos == (iota((TP, 192), 1) & 63), 1.0, 0.0).astype(BF)
-        col_pos = pos_of(iota((192, TP), 1), r, c)
-        ecol[...] = jnp.where(col_pos == (iota((192, TP), 0) & 63), 1.0, 0.0).astype(BF)
-        acc[...] = jnp.zeros_like(acc)
-
+def attn_masks(r, c, last, mask, ecol, erow):
+    tq, tk = iota((TP, TP), 0), iota((TP, TP), 1)
+    wq_, lq = group_of(tq, r, c, last)
+    wk_, lk = group_of(tk, r, c, last)
+    seen = jnp.where(wq_ == wk_, jnp.where(lq == lk, 0.0, -100.0), NEG)
+    mask[...] = jnp.where(tk < TOK, seen, NEG)
+    row_pos = pos_of(iota((TP, 192), 0), r, c)
+    erow[...] = jnp.where(row_pos == (iota((TP, 192), 1) & 63), 1.0, 0.0).astype(BF)
+    col_pos = pos_of(iota((192, TP), 1), r, c)
+    ecol[...] = jnp.where(col_pos == (iota((192, TP), 0) & 63), 1.0, 0.0).astype(BF)
+
+
+def cols(start):
+    return pl.ds(pl.multiple_of(start, GRP), GRP)
+
+
+def attn_group(g, normed, wqkv, wo, bias, mask, ecol, erow, qkv, probs, acc):
     n = normed[...]
-    q = dot(n, wq[...]).astype(BF)
-    k = dot(n, wk[...]).astype(BF)
-    v = dot(n, wv[...]).astype(BF)
-    q_out[...] = q
-    k_out[...] = k
-    v_out[...] = v
-    wide = dot(jnp.concatenate(split3(bias[...].reshape(8 * 64, 64)), axis=1), ecol[...])
+    q = dot(n, wqkv[:, cols(g * GRP)]).astype(BF)
+    k = dot(n, wqkv[:, cols(C + g * GRP)]).astype(BF)
+    v = dot(n, wqkv[:, cols(2 * C + g * GRP)]).astype(BF)
+    qkv[0, g] = q
+    qkv[1, g] = k
+    qkv[2, g] = v
+    wide = dot(jnp.concatenate(split3(bias[pl.ds(g * 8, 8)].reshape(8 * 64, 64)), axis=1), ecol[...])
     w_hi, w_mid, w_lo = split3(wide)
     lane_head = iota((TP, GRP), 1) >> 5
     mixed = jnp.zeros((TP, GRP), F32)
@@ -145,13 +140,9 @@
         s = s + dot(erow[...], jnp.concatenate([w_hi[part], w_mid[part], w_lo[part]], axis=0)) + mask[...]
         e = jnp.exp(s - jnp.max(s, axis=-1, keepdims=True))
         p = (e / jnp.sum(e, axis=-1, keepdims=True)).astype(BF)
-        p_out[h * TP:(h + 1) * TP, :] = p
+        probs[pl.ds(pl.multiple_of((g * 8 + h) * TP, 16), TP), :] = p
         mixed = jnp.where(mine, dot(p, v), mixed)
-    acc[...] += dot(mixed.astype(BF), wo[...])
-
-    @pl.when(g == 3)
-    def _():
-        att[...] = acc[...].astype(BF)
+    acc[...] += dot(mixed.astype(BF), wo[pl.ds(pl.multiple_of(g * GRP, GRP), GRP), :])
 
 
 def attn_bwd(scal, own, halo, wq, wk, wv, wo, q_in, k_in, v_in, p_in, d_shift, d_att, acc):
@@ -164,7 +155,7 @@
         d_att[HALO:, :] = own[HALO:, :]
         acc[...] = jnp.zeros_like(acc)
 
-    q, k, v = q_in[...], k_in[...], v_in[...]
+    q, k, v = q_in[0, 0], k_in[0, 0], v_in[0, 0]
     d_mixed = dot(d_att[...], wo[...], 1, 1).astype(BF).astype(F32)
     q32 = q.astype(F32)
     lane_head = iota((TP, GRP), 1) >> 5
@@ -190,8 +181,7 @@
         d_shift[...] = acc[...].astype(BF)
 
 
-def route(scal, x, att, halo, choice_col, choice_row, after_out, slots, table_out):
-    r = scal[0]
+def route(r, x, att, halo, choice_col, choice_row, after_out, slots, table_out):
     top = jnp.where(iota((HALO, C), 0) < 14 * r, halo[...].astype(F32), att[:HALO, :].astype(F32))
     after_out[:HALO, :] = (x[:HALO, :].astype(F32) + top).astype(BF)
     after_out[HALO:, :] = (x[HALO:, :].astype(F32) + att[HALO:, :].astype(F32)).astype(BF)
@@ -223,7 +213,7 @@
     return jnp.concatenate([dot(table, low.astype(BF)), dot(table, high.astype(BF))], axis=1)
 
 
-def merge_mid(after, ret, table_in, gate_in, parts, mn_out, d_block_out, slots, spread):
+def merge_mid(after, ret, table_in, gate_in, parts, tail, mn_out, d_block_out, slots, spread):
     table = table_in[...]
     gate = gate_in[...]
     block = (after[...].astype(F32) + gate * gathered(ret, table)).astype(BF)
@@ -238,12 +228,14 @@
     unit = [v * scale for v in cent]
     for q in range(4):
         mn_out[:, q * C:(q + 1) * C] = unit[q].astype(BF)
+    tails = jnp.sum(tail[...].astype(F32), axis=0)
     cots = []
     for q in range(4):
         tot = parts[0, :, q * C:(q + 1) * C].astype(F32)
         for s in range(1, 8):
             tot = tot + parts[s, :, q * C:(q + 1) * C].astype(F32)
-        cots.append(tot)
+        last = jnp.concatenate([tails[4 * q + i:4 * q + i + 1, :] for i in range(4)], axis=1)
+        cots.append(jnp.concatenate([tot, last], axis=0))
     mean_cot = sum(jnp.sum(v, axis=-1, keepdims=True) for v in cots) * inv
     mean_dot = sum(jnp.sum(v * u, axis=-1, keepdims=True) for v, u in zip(cots, unit)) * inv
     spread[...] = jnp.zeros_like(spread)
@@ -272,37 +264,35 @@
     ).astype(BF)
 
 
-def expert_fwd(slots, *refs):
-    ups, downs = refs[:4], refs[4:8]
-    flat, act_out, slope_out, packed = refs[8:]
-    low, high = unpack_rows(slots[...], 32)
+def expert_chunk(j, recv, part, ups, downs, flat, act_out, slope_out):
+    here = pl.ds(8 * j, 8)
+    rows_here = pl.ds(256 * j, 256)
+    low, high = unpack_rows(recv[:, here].reshape(32, 16, HC), 32)
+    rows = jnp.concatenate([low, high], axis=1).astype(BF)
+    flat[rows_here, :] = rows
+    total = jnp.zeros((256, C), F32)
+    for k in range(4):
+        pre = dot(rows, ups[k])
+        cdf = 0.5 * (1.0 + lax.erf(pre * np.float32(2.0 ** -0.5)))
+        act = (pre * cdf).astype(BF)
+        slope = cdf + pre * jnp.exp(-0.5 * pre * pre) * np.float32((2.0 * np.pi) ** -0.5)
+        act_out[rows_here, k * 256:(k + 1) * 256] = act
+        slope_out[rows_here, k * 256:(k + 1) * 256] = slope.astype(BF)
+        total = total + dot(act, downs[k])
+    part[:, here] = pack_rows(total[:, :HC], total[:, HC:], 32).reshape(4, 8, 16, HC)
+
+
+def expert_bwd(slots, slope, ups, downs, flat, d_pre_out, packed):
+    low, high = unpack_rows(slots[...].reshape(32, 16, HC), 32)
     rows = jnp.concatenate([low, high], axis=1).astype(BF)
     flat[...] = rows
     total = jnp.zeros((256, C), F32)
     for k in range(4):
-        pre = dot(rows, ups[k][...])
-        cdf = 0.5 * (1.0 + lax.erf(pre * np.float32(2.0 ** -0.5)))
-        act = (pre * cdf).astype(BF)
-        slope = cdf + pre * jnp.exp(-0.5 * pre * pre) * np.float32((2.0 * np.pi) ** -0.5)
-        act_out[:, k * 256:(k + 1) * 256] = act
-        slope_out[:, k * 256:(k + 1) * 256] = slope.astype(BF)
-        total = total + dot(act, downs[k][...])
-    packed[...] = pack_rows(total[:, :HC], total[:, HC:], 32)
-
-
-def expert_bwd(slots, slope, *refs):
-    ups, downs = refs[:4], refs[4:8]
-    flat, d_pre_out, packed = refs[8:]
-    low, high = unpack_rows(slots[...], 32)
-    rows = jnp.concatenate([low, high], axis=1).astype(BF)
-    flat[...] = rows
-    total = jnp.zeros((256, C), F32)
-    for k in range(4):
-        cols = slice(k * 256, (k + 1) * 256)
-        d_pre = (slope[:, cols].astype(F32) * dot(rows, downs[k][...], 1, 1)).astype(BF)
-        d_pre_out[:, cols] = d_pre
-        total = total + dot(d_pre, ups[k][...], 1, 1)
-    packed[...] = pack_rows(total[:, :HC], total[:, HC:], 32)
+        span = slice(k * 256, (k + 1) * 256)
+        d_pre = (slope[:, span].astype(F32) * dot(rows, downs[k], 1, 1)).astype(BF)
+        d_pre_out[:, span] = d_pre
+        total = total + dot(d_pre, ups[k], 1, 1)
+    packed[...] = pack_rows(total[:, :HC], total[:, HC:], 32).reshape(4, 8, 16, HC)
 
 
 def expert_grads(act, d_rows, rows, d_pre, down_out, up_out):
@@ -330,7 +320,7 @@
     return (s, z * 4 + y * 2 + c)
 
 
-def greet(s, z, y, c):
+def greet(s, z, y, c, total=64):
     barrier = pltpu.get_barrier_semaphore()
     mine = s * 4 + z
 
@@ -343,7 +333,245 @@
     lax.fori_loop(1, 32, hail, 0)
     pl.semaphore_signal(barrier, inc=1, device_id=at(s, z, 1 - y, c), device_id_type=MESH)
     pl.semaphore_signal(barrier, inc=1, device_id=at(s, z, y, 1 - c), device_id_type=MESH)
-    pl.semaphore_wait(barrier, 64)
+    pl.semaphore_wait(barrier, total)
+
+
+def remote(src, dst, send, recv, device):
+    return pltpu.make_async_remote_copy(
+        src_ref=src, dst_ref=dst, send_sem=send, recv_sem=recv, device_id=device, device_id_type=MESH
+    )
+
+
+def await_bytes(ref, sem):
+    pltpu.make_async_copy(ref, ref, sem).wait()
+
+
+SLOT_SEMS = [
+    pltpu.SemaphoreType.DMA,
+    pltpu.SemaphoreType.DMA((2, 4)),
+    pltpu.SemaphoreType.DMA((2, 4)),
+    pltpu.SemaphoreType.DMA((2, 4)),
+    pltpu.SemaphoreType.DMA((2, 4)),
+    pltpu.SemaphoreType.DMA((2, 4)),
+    pltpu.SemaphoreType.DMA,
+    pltpu.SemaphoreType.DMA,
+]
+
+
+def slots_through(place, slots, recv, part, other, total, ret, sems, compute):
+    s, z, y, c = place
+    mine = s * 4 + z
+    send, arrive, f_send, f_recv, p_send, p_recv, r_send, r_recv = sems
+    pair = at(s, z, y, 1 - c)
+
+    def to_peer(k, peer, yy):
+        remote(slots.at[peer], recv.at[y * 2 + c, k], send, arrive.at[y, k // 8], at(peer // 4, peer % 4, yy, c)).start()
+
+    def push(k, carry):
+        peer = (mine + k) % 32
+        to_peer(k, peer, y)
+        to_peer(k, peer, 1 - y)
+        return carry
+
+    pltpu.make_async_copy(slots.at[mine], recv.at[y * 2 + c, 0], arrive.at[y, 0]).start()
+    to_peer(0, mine, 1 - y)
+    lax.fori_loop(1, 32, push, 0)
+    forwards, partials = {}, {}
+
+    def forward(j):
+        for yy in range(2):
+            block = recv.at[yy * 2 + c, pl.ds(8 * j, 8)]
+            await_bytes(block, arrive.at[yy, j])
+            forwards[yy, j] = remote(block, block, f_send.at[yy, j], f_recv.at[yy, j], pair)
+            forwards[yy, j].start()
+
+    def work(j):
+        for yy in range(2):
+            forwards[yy, j].wait_recv()
+        compute(j)
+        for yy in range(2):
+            here = pl.ds(8 * j, 8)
+            partials[yy, j] = remote(
+                part.at[yy * 2 + (1 - c), here], other.at[yy, here], p_send.at[yy, j], p_recv.at[yy, j], pair
+            )
+            partials[yy, j].start()
+
+    def give(k, yy):
+        peer = (mine - k + 32) % 32
+        remote(total.at[yy, k], ret.at[y, mine], r_send, r_recv, at(peer // 4, peer % 4, yy, c)).start()
+
+    def give_both(k, carry):
+        give(k, 1 - y)
+        give(k, y)
+        return carry
+
+    def back(j):
+        here = pl.ds(8 * j, 8)
+        for yy in range(2):
+            partials[yy, j].wait_recv()
+            total[yy, here] = (part[yy * 2 + c, here].astype(F32) + other[yy, here].astype(F32)).astype(BF)
+        if j == 0:
+            give(0, 1 - y)
+            pltpu.make_async_copy(total.at[y, 0], ret.at[y, mine], r_recv).start()
+        lax.fori_loop(max(1, 8 * j), 8 * j + 8, give_both, 0)
+
+    forward(0)
+    forward(1)
+    work(0)
+    forward(2)
+    work(1)
+    back(0)
+    forward(3)
+    work(2)
+    back(1)
+    work(3)
+    back(2)
+    back(3)
+
+    def finish_sends():
+        for copy in list(forwards.values()) + list(partials.values()):
+            copy.wait_send()
+        for sem in (send, r_send):
+            await_bytes(total.at[0], sem)
+            await_bytes(total.at[0, pl.ds(0, 31)], sem)
+
+    await_bytes(ret, r_recv)
+    return finish_sends
+
+
+def front(
+    scal, x, bias, choice_col, choice_row, gate, grad48, grad_tail, qkv_weight, out_weight, expert_up, expert_down, reduce_weight,
+    after, table, merge_norm, d_block, d_slots, qkv_out, probs_out, flat_out, act_out, slope_out, up_out, down_out,
+    halo, halo2, normed, mask, ecol, erow, acc, att, wqkv, wo, wred, qkv, probs,
+    d_send, d_recv, t_wide, t_send, t_recv, ups, downs, relay_up, relay_down,
+    slots, recv, part, other, total, ret, flat, act, slope, spread,
+    io_sem, halo_sem, w_send, w_recv, d_sem, *slot_sems,
+):
+    place = coords()
+    s, z, y, c = place
+    row = z * 4 + y * 2 + c
+    r, cc, last = scal[0], scal[1], scal[2]
+    ins = [
+        pltpu.make_async_copy(reduce_weight, wred, io_sem.at[0]),
+        pltpu.make_async_copy(qkv_weight, wqkv, io_sem.at[1]),
+        pltpu.make_async_copy(out_weight, wo, io_sem.at[2]),
+        pltpu.make_async_copy(expert_up.at[z], ups.at[0], io_sem.at[3]),
+        pltpu.make_async_copy(expert_down.at[z], downs.at[0], io_sem.at[4]),
+    ]
+    for copy in ins:
+        copy.start()
+    greet_all(place)
+
+    nxt = (s, (row + 1) % 16)
+    prv = (s, (row + 15) % 16)
+    z_up, z_down = at(s, (z + 1) % 4, y, c), at(s, (z + 3) % 4, y, c)
+    halo_copy = remote(x.at[pl.ds(0, HALO)], halo, halo_sem.at[0], halo_sem.at[1], prv)
+    halo_copy.start()
+    weights = [
+        remote(expert_up.at[(z + 2) % 4], relay_up, w_send.at[0], w_recv.at[0], z_up),
+        remote(expert_down.at[(z + 2) % 4], relay_down, w_send.at[1], w_recv.at[1], z_down),
+        remote(expert_up.at[(z + 1) % 4], ups.at[1], w_send.at[2], w_recv.at[2], z_up),
+        remote(expert_up.at[(z + 3) % 4], ups.at[3], w_send.at[3], w_recv.at[3], z_down),
+        remote(expert_down.at[(z + 1) % 4], downs.at[1], w_send.at[4], w_recv.at[4], z_up),
+        remote(expert_down.at[(z + 3) % 4], downs.at[3], w_send.at[5], w_recv.at[5], z_down),
+    ]
+    for copy in weights:
+        copy.start()
+    relayed = [
+        remote(relay_up, ups.at[2], w_send.at[6], w_recv.at[6], z_up),
+        remote(relay_down, downs.at[2], w_send.at[7], w_recv.at[7], z_down),
+    ]
+
+    ins[0].wait()
+    for half in range(4):
+        span = pl.ds(half * C, C)
+        d_send[:, :, span] = dot(grad48[...], wred[span, :], 1, 1).astype(BF).reshape(8, 48, C)
+        tail = dot(grad_tail[...], wred[span, :], 1, 1)
+        for i in range(4):
+            t_wide[:, 4 * half + i, :] = tail[:8, i * 256:(i + 1) * 256]
+    t_send[...] = t_wide[...].astype(BF)
+    gifts = []
+    for k in range(1, 8):
+        peer = (s + k) % 8
+        gifts.append(remote(d_send.at[peer], d_recv.at[s], d_sem.at[0, k], d_sem.at[1, k], at(peer, z, y, c)))
+        gifts.append(remote(t_send.at[peer], t_recv.at[s], d_sem.at[2, k], d_sem.at[3, k], at(peer, z, y, c)))
+    for copy in gifts:
+        copy.start()
+    own = [
+        pltpu.make_async_copy(d_send.at[s], d_recv.at[s], io_sem.at[5]),
+        pltpu.make_async_copy(t_send.at[s], t_recv.at[s], io_sem.at[6]),
+    ]
+    for copy in own:
+        copy.start()
+
+    attn_masks(r, cc, last, mask, ecol, erow)
+    normed[HALO:, :] = norm_parts(x[HALO:, :].astype(F32))[0].astype(BF)
+    acc[...] = jnp.zeros_like(acc)
+    halo_copy.wait_recv()
+    top = jnp.where(iota((HALO, C), 0) < 14 * r, halo[...].astype(F32), x[:HALO, :].astype(F32))
+    normed[:HALO, :] = norm_parts(top)[0].astype(BF)
+    ins[1].wait()
+    ins[2].wait()
+
+    def group(g, carry):
+        attn_group(g, normed, wqkv, wo, bias, mask, ecol, erow, qkv, probs, acc)
+        return carry
+
+    lax.fori_loop(0, 3, group, 0)
+    for arrived, onward in zip(weights, relayed):
+        arrived.wait_recv()
+        onward.start()
+    lax.fori_loop(3, 4, group, 0)
+    att[...] = acc[...].astype(BF)
+    halo2_copy = remote(att.at[pl.ds(0, HALO)], halo2, halo_sem.at[2], halo_sem.at[3], nxt)
+    halo2_copy.start()
+    outs = [
+        pltpu.make_async_copy(qkv, qkv_out, io_sem.at[7]),
+        pltpu.make_async_copy(probs, probs_out, io_sem.at[8]),
+    ]
+    for copy in outs:
+        copy.start()
+    halo2_copy.wait_recv()
+    route(r, x, att, halo2, choice_col, choice_row, after, slots, table)
+
+    def compute(j):
+        if j == 0:
+            for copy in weights[2:] + relayed:
+                copy.wait_recv()
+            ins[3].wait()
+            ins[4].wait()
+        expert_chunk(j, recv, part, ups, downs, flat, act, slope)
+
+    finish_sends = slots_through(place, slots, recv, part, other, total, ret, slot_sems, compute)
+    more = [
+        pltpu.make_async_copy(flat, flat_out, io_sem.at[9]),
+        pltpu.make_async_copy(act, act_out, io_sem.at[10]),
+        pltpu.make_async_copy(slope, slope_out, io_sem.at[11]),
+        pltpu.make_async_copy(ups, up_out, io_sem.at[12]),
+        pltpu.make_async_copy(downs, down_out, io_sem.at[13]),
+    ]
+    for copy in more:
+        copy.start()
+    for k in range(1, 8):
+        gifts[2 * k - 2].wait_recv()
+        gifts[2 * k - 1].wait_recv()
+    for copy in own:
+        copy.wait()
+    merge_mid(after, ret, table, gate, d_recv, t_recv, merge_norm, d_block, d_slots, spread)
+    for copy in outs + more:
+        copy.wait()
+    finish_sends()
+    for copy in weights + relayed + gifts + [halo_copy, halo2_copy]:
+        copy.wait_send()
+
+
+def greet_all(place):
+    s, z, y, c = place
+    barrier = pltpu.get_barrier_semaphore()
+    row = z * 4 + y * 2 + c
+    pl.semaphore_signal(barrier, inc=1, device_id=(s, (row + 1) % 16), device_id_type=MESH)
+    pl.semaphore_signal(barrier, inc=1, device_id=(s, (row + 15) % 16), device_id_type=MESH)
+    greet(s, z, y, c, 66)
 
 
 def dispatch_kernel(src, out, send_sem, recv_sem, pair_send, pair_recv):
@@ -355,14 +583,14 @@
         peer = (mine + k) % 32
         for yy in range(2):
             pltpu.make_async_remote_copy(
-                src_ref=src.at[peer], dst_ref=out.at[y * 2 + c, mine], send_sem=send_sem, recv_sem=recv_sem.at[y],
+                src_ref=src.at[peer], dst_ref=out.at[y * 2 + c, k], send_sem=send_sem, recv_sem=recv_sem.at[y],
                 device_id=at(peer // 4, peer % 4, (y + yy) % 2, c), device_id_type=MESH,
             ).start()
         return carry
 
-    pltpu.make_async_copy(src.at[mine], out.at[y * 2 + c, mine], recv_sem.at[y]).start()
+    pltpu.make_async_copy(src.at[mine], out.at[y * 2 + c, 0], recv_sem.at[y]).start()
     pltpu.make_async_remote_copy(
-        src_ref=src.at[mine], dst_ref=out.at[y * 2 + c, mine], send_sem=send_sem, recv_sem=recv_sem.at[y],
+        src_ref=src.at[mine], dst_ref=out.at[y * 2 + c, 0], send_sem=send_sem, recv_sem=recv_sem.at[y],
         device_id=at(s, z, 1 - y, c), device_id_type=MESH,
     ).start()
     lax.fori_loop(1, 32, push, 0)
@@ -413,13 +641,14 @@
         copy.start()
         pairs.append(copy)
 
-    def add(yy, peer):
-        summed = part[yy * 2 + c, peer].astype(F32) + other[yy, peer].astype(F32)
-        total[yy, peer] = summed.astype(BF)
-
-    def ship(yy, peer):
+    def add(yy, k):
+        summed = part[yy * 2 + c, k].astype(F32) + other[yy, k].astype(F32)
+        total[yy, k] = summed.astype(BF)
+
+    def ship(yy, k):
+        peer = (mine - k + 32) % 32
         pltpu.make_async_remote_copy(
-            src_ref=total.at[yy, peer], dst_ref=out.at[y, mine], send_sem=send_sem, recv_sem=recv_sem,
+            src_ref=total.at[yy, k], dst_ref=out.at[y, mine], send_sem=send_sem, recv_sem=recv_sem,
             device_id=at(peer // 4, peer % 4, yy, c), device_id_type=MESH,
         ).start()
 
@@ -427,18 +656,17 @@
         copy.wait_recv()
 
     def push(k, carry):
-        peer = (mine + k) % 32
-        add(1 - y, peer)
-        ship(1 - y, peer)
-        add(y, peer)
-        ship(y, peer)
+        add(1 - y, k)
+        ship(1 - y, k)
+        add(y, k)
+        ship(y, k)
         return carry
 
     lax.fori_loop(1, 32, push, 0)
-    add(1 - y, mine)
-    ship(1 - y, mine)
-    add(y, mine)
-    pltpu.make_async_copy(total.at[y, mine], out.at[y, mine], recv_sem).start()
+    add(1 - y, 0)
+    ship(1 - y, 0)
+    add(y, 0)
+    pltpu.make_async_copy(total.at[y, 0], out.at[y, mine], recv_sem).start()
     for copy in pairs:
         copy.wait_send()
     pltpu.make_async_copy(total, total, recv_sem).wait()
@@ -519,20 +747,9 @@
     choice = jnp.pad(expert_choice.reshape(TOK), (0, TP - TOK), constant_values=-1000)
     gate = jnp.pad(combine_weight.reshape(TOK, 1), ((0, TP - TOK), (0, 0)))
 
-    below = row_shift(x[:HALO], -1)
-    ups, downs = [], []
-    for k in range(4):
-        expert = (z + k) % 4
-        up_k = lax.dynamic_index_in_dim(expert_up, expert, 0, keepdims=False)
-        down_k = lax.dynamic_index_in_dim(expert_down, expert, 0, keepdims=False)
-        ups.append(z_shift(up_k, k) if k else up_k)
-        downs.append(z_shift(down_k, k) if k else down_k)
-
-    d_parts = jnp.einsum(
-        "nkd,cd->nkc", merged_grad.reshape(8, 49, -1), reduce_weight, preferred_element_type=F32
-    ).astype(BF)
-    d_parts = lax.all_to_all(d_parts, "scene", split_axis=0, concat_axis=0, tiled=True)
-
+    grads49 = merged_grad.reshape(8, 49, -1)
+    grad48 = grads49[:, :48].reshape(8 * 48, -1)
+    grad_tail = jnp.pad(grads49[:, 48], ((0, 8), (0, 0)))
     bias = jnp.dot(position_bias, jnp.asarray(bias_pairs()), precision=lax.Precision.HIGHEST).reshape(32, 64, 64)
 
     full = lambda shape: pl.BlockSpec(shape, lambda g: (0,) * len(shape))
@@ -540,62 +757,56 @@
     wo_spec = pl.BlockSpec((GRP, C), lambda g: (g, 0))
     head_spec = pl.BlockSpec((TP, GRP), lambda g: (0, g))
     prob_spec = pl.BlockSpec((8 * TP, TP), lambda g: (g, 0))
-    att, q, k, v, probs = pl.pallas_call(
-        attn_fwd,
-        grid=(4,),
-        out_shape=[sds((TP, C), BF)] * 4 + [sds((32 * TP, TP), BF)],
-        in_specs=[SM, full((TP, C)), full((HALO, C)), w_spec(0), w_spec(1), w_spec(2), wo_spec,
-                  pl.BlockSpec((8, 64, 64), lambda g: (g, 0, 0))],
-        out_specs=[full((TP, C)), head_spec, head_spec, head_spec, prob_spec],
-        scratch_shapes=[pltpu.VMEM((TP, C), BF), pltpu.VMEM((TP, TP), F32), pltpu.VMEM((192, TP), BF),
-                        pltpu.VMEM((TP, 192), BF), pltpu.VMEM((TP, C), F32)],
-        compiler_params=params(),
-        cost_estimate=cost(6 << 30, 14 << 20),
-        name="attn_fwd",
-    )(scal, x, below, qkv_weight, qkv_weight, qkv_weight, out_weight, bias)
-
-    above = row_shift(att[:HALO], 1)
-    after, slots, table = whole(
-        route,
-        [sds((TP, C), BF), sds((32, 16, HC), BF), sds((TP, 256), BF)],
-        (scal, x, att, above, choice.reshape(TP, 1), choice.reshape(1, TP)),
-        [SM] + [VM] * 5, flops=1 << 30, nbytes=4 << 20,
-    )
-    slot_in = dispatch(slots).reshape(128, 16, HC)
-
-    slot_spec = pl.BlockSpec((32, 16, HC), lambda g: (g, 0, 0))
+    after, table, merge_norm, d_block, d_slots, qkv, probs, flat_in, act, slope, ups, downs = pl.pallas_call(
+        front,
+        out_shape=[
+            sds((TP, C), BF), sds((TP, 256), BF), sds((49, 4 * C), BF), sds((TP, C), F32), sds((32, 16, HC), BF),
+            sds((3, 4, TP, GRP), BF), sds((32 * TP, TP), BF), sds((C, C), BF), sds((C, C), BF), sds((C, C), BF),
+            sds((4, C, 256), BF), sds((4, 256, C), BF),
+        ],
+        in_specs=[SM] + [VM] * 7 + [HB] * 5,
+        out_specs=[VM] * 5 + [HB] * 7,
+        scratch_shapes=[
+            pltpu.VMEM((HALO, C), BF), pltpu.VMEM((HALO, C), BF), pltpu.VMEM((TP, C), BF), pltpu.VMEM((TP, TP), F32),
+            pltpu.VMEM((192, TP), BF), pltpu.VMEM((TP, 192), BF), pltpu.VMEM((TP, C), F32), pltpu.VMEM((TP, C), BF),
+            pltpu.VMEM((C, 3 * C), BF), pltpu.VMEM((C, C), BF), pltpu.VMEM((4 * C, 256), BF),
+            pltpu.VMEM((3, 4, TP, GRP), BF), pltpu.VMEM((32 * TP, TP), BF),
+            pltpu.VMEM((8, 48, 4 * C), BF), pltpu.VMEM((8, 48, 4 * C), BF), pltpu.VMEM((8, 16, 256), F32),
+            pltpu.VMEM((8, 16, 256), BF), pltpu.VMEM((8, 16, 256), BF),
+            pltpu.VMEM((4, C, 256), BF), pltpu.VMEM((4, 256, C), BF), pltpu.VMEM((C, 256), BF), pltpu.VMEM((256, C), BF),
+            pltpu.VMEM((32, 16, HC), BF), pltpu.VMEM((4, 32, 16, HC), BF), pltpu.VMEM((4, 32, 16, HC), BF),
+            pltpu.VMEM((2, 32, 16, HC), BF), pltpu.VMEM((2, 32, 16, HC), BF), pltpu.VMEM((2, 32, 16, HC), BF),
+            pltpu.VMEM((C, C), BF), pltpu.VMEM((C, C), BF), pltpu.VMEM((C, C), BF), pltpu.VMEM((256, C), F32),
+            pltpu.SemaphoreType.DMA((14,)), pltpu.SemaphoreType.DMA((4,)), pltpu.SemaphoreType.DMA((8,)),
+            pltpu.SemaphoreType.DMA((8,)), pltpu.SemaphoreType.DMA((4, 8)), *SLOT_SEMS,
+        ],
+        compiler_params=params(collective_id=2, has_side_effects=True),
+        cost_estimate=cost(12 << 30, 60 << 20),
+        name="front",
+    )(scal, x, bias, choice.reshape(TP, 1), choice.reshape(1, TP), gate, grad48, grad_tail, qkv_weight, out_weight,
+      expert_up, expert_down, reduce_weight)
+
+    full = lambda shape: pl.BlockSpec(shape, lambda g: (0,) * len(shape))
+    w_spec = lambda which: pl.BlockSpec((C, GRP), lambda g: (0, 4 * which + g))
+    wo_spec = pl.BlockSpec((GRP, C), lambda g: (g, 0))
+    head_spec = lambda which: pl.BlockSpec((1, 1, TP, GRP), lambda g: (which, g, 0, 0))
+    prob_spec = pl.BlockSpec((8 * TP, TP), lambda g: (g, 0))
+    slot_spec = pl.BlockSpec((4, 8, 16, HC), lambda g: (0, g, 0, 0))
     row_spec = pl.BlockSpec((256, C), lambda g: (g, 0))
-    weight_specs = [full((C, 256))] * 4 + [full((256, C))] * 4
-    flat_in, act, slope, part = pl.pallas_call(
-        expert_fwd,
-        grid=(4,),
-        out_shape=[sds((C, C), BF)] * 3 + [sds((128, 16, HC), BF)],
-        in_specs=[slot_spec] + weight_specs,
-        out_specs=[row_spec] * 3 + [slot_spec],
-        compiler_params=params(),
-        cost_estimate=cost(4 << 30, 14 << 20),
-        name="expert_fwd",
-    )(slot_in, *ups, *downs)
-    ret = combine(part.reshape(4, 32, 16, HC))
-
-    merge_norm, d_block, d_slots = whole(
-        merge_mid,
-        [sds((49, 4 * C), BF), sds((TP, C), F32), sds((32, 16, HC), BF)],
-        (after, ret, table, gate, d_parts),
-        [VM] * 5, scratch=[pltpu.VMEM((256, C), F32)], flops=2 << 30, nbytes=8 << 20,
-    )
-    d_slot_in = dispatch(d_slots).reshape(128, 16, HC)
+    weight_specs = [full((4, C, 256)), full((4, 256, C))]
+
+    d_slot_in = dispatch(d_slots)
     flat_d, d_pre, d_part = pl.pallas_call(
         expert_bwd,
         grid=(4,),
-        out_shape=[sds((C, C), BF)] * 2 + [sds((128, 16, HC), BF)],
+        out_shape=[sds((C, C), BF)] * 2 + [sds((4, 32, 16, HC), BF)],
         in_specs=[slot_spec, row_spec] + weight_specs,
         out_specs=[row_spec] * 2 + [slot_spec],
         compiler_params=params(),
         cost_estimate=cost(4 << 30, 14 << 20),
         name="expert_bwd",
-    )(d_slot_in, slope, *ups, *downs)
-    d_ret = combine(d_part.reshape(4, 32, 16, HC))
+    )(d_slot_in, slope, ups, downs)
+    d_ret = combine(d_part)
 
     col_spec = pl.BlockSpec((C, 256), lambda g: (0, g))
     down_parts, up_parts = pl.pallas_call(
@@ -621,13 +832,13 @@
         grid=(4,),
         out_shape=sds((TP, C), BF),
         in_specs=[SM, full((TP, C)), full((HALO, C)), w_spec(0), w_spec(1), w_spec(2), wo_spec,
-                  head_spec, head_spec, head_spec, prob_spec],
+                  head_spec(0), head_spec(1), head_spec(2), prob_spec],
         out_specs=full((TP, C)),
         scratch_shapes=[pltpu.VMEM((TP, C), BF), pltpu.VMEM((TP, C), F32)],
         compiler_params=params(),
         cost_estimate=cost(8 << 30, 14 << 20),
         name="attn_bwd",
-    )(scal, d_att, d_below, qkv_weight, qkv_weight, qkv_weight, out_weight, q, k, v, probs)
+    )(scal, d_att, d_below, qkv_weight, qkv_weight, qkv_weight, out_weight, qkv, qkv, qkv, probs)
     d_above = row_shift(d_shift[:HALO], 1)
     (grad,) = whole(
         finish, [sds((TP, C), BF)], (scal, x, d_after, d_shift, d_above), [SM] + [VM] * 4,

time: 363 us -> 290 us (0.80); the launches traced: 357 us -> 288 us
  starting transfers between devices: 30.4 us -> 5.95 us
  Pallas kernels: 241 us -> 219 us
  waiting for transfers between devices: 40 us -> 21.8 us
    pallas_call x2 -> x1, Pallas kernels: 31.3 us -> 107 us  [local(): pl.pallas_call(front, out_shape=[sds((TP, C), BF), sds((TP, 256), BF), sd...]
    pallas_call x2 -> x1, Pallas kernels: 81.1 us -> 25 us  [dispatch(): pl.pallas_call(dispatch_kernel, out_shape=sds((4, 32, 16, HC), BF), in_sp...]
    pallas_call x2 -> x1, Pallas kernels: 69.5 us -> 35.4 us  [combine(): pl.pallas_call(combine_kernel, out_shape=sds((2, 32, 16, HC), BF), in_spe...]
    ppermute x4 -> x2, waiting for transfers between devices: 24.1 us -> 5.79 us  [row_shift(): return lax.ppermute(value, 'row', pairs)]
    ppermute x12 -> x6, starting transfers between devices: 16.2 us -> 5.77 us  [z_shift(): return lax.ppermute(value, 'row', pairs)]
    pallas_call x4 -> x2, Pallas kernels: 14.6 us -> 6.12 us  [whole(): pl.pallas_call(kernel, out_shape=out_shape, in_specs=specs, out_specs=[VM...]
    all_to_all x1 -> x0, starting transfers between devices: 7.15 us -> none  [local(): lax.all_to_all(d_parts, 'scene', split_axis=0, concat_axis=0, tiled=True)]
    ppermute x4 -> x2, starting transfers between devices: 7.09 us -> 0.15 us  [row_shift(): return lax.ppermute(value, 'row', pairs)]
  transfers between devices with their start and end apart: 18 -> 9, of which waited for: 3 -> 2; matrix products, arithmetic and copies ran while one was open for 6% -> 3% of each run, Pallas kernels for 66% -> 39%
where the time goes in v2:
time: 290 us; the launch traced here: 288 us
  Pallas kernels  219 us (76%)
  waiting for transfers between devices  21.8 us (8%)
  local copies, waits for them, and re-layouts  18 us (6%)
  between operations  14.2 us (5%)
  matrix products  7.67 us (3%)
  starting transfers between devices  5.95 us (2%)
    pallas_call x1, Pallas kernels, local(): pl.pallas_call(front, out_shape=[sds((TP, C), BF), sds((TP, 256), BF), sd...  107 us
    pallas_call x1, Pallas kernels, combine(): pl.pallas_call(combine_kernel, out_shape=sds((2, 32, 16, HC), BF), in_spe...  35.4 us
    pallas_call x1, Pallas kernels, dispatch(): pl.pallas_call(dispatch_kernel, out_shape=sds((4, 32, 16, HC), BF), in_sp...  25 us
    pallas_call x1, Pallas kernels, local(): pl.pallas_call(attn_bwd, grid=(4,), out_shape=sds((TP, C), BF), in_specs=...  19.7 us
    ppermute x6, waiting for transfers between devices, z_shift(): return lax.ppermute(value, 'row', pairs)  16 us
    pallas_call x1, Pallas kernels, local(): pl.pallas_call(expert_bwd, grid=(4,), out_shape=[sds((C, C), BF)] * 2 + [...  10.7 us
    pallas_call x1, Pallas kernels, local(): pl.pallas_call(expert_grads, grid=(4,), out_shape=[sds((4, 256, C), BF),...  8.72 us
    pallas_call x2, Pallas kernels, whole(): pl.pallas_call(kernel, out_shape=out_shape, in_specs=specs, out_specs=[VM...  6.12 us
  transfers between devices with their start and end apart: 9, of which 2 were waited for; matrix products, arithmetic and copies ran while one was open for 3% of the time, Pallas kernels for 39%

profile of v2, /device:TPU:0, one launch (start us, length us, event | category | flops | bytes accessed | tf_op | source)
XLA Modules:
  0.0 288.5 jit_solution(2426017120258241127)
XLA Ops:
  7.9 0.9 slice.55
  12.0 1.1 reshape.39
  14.6 3.8 %convolution_bitcast_fusion = f32[32,4096]{1,0:T(8,128)S(1)} fusion(f32[169,4096]{1,0:T(8,128)} %constant.31.clone, f32[32,169]{1,0:T(8,128)S(1)} %copy-done), kind=kOutput, calls=%fused_computation | convolution fusion | flops 265814016 | bytes 3314816 | tf_op jit(solution)/shard_map/dot_general | solution.py:753
  18.4 1.4 reshape.40.bias
  21.1 107.2 %front.1 = (bf16[208,1024]{1,0:T(8,128)(2,1)}, bf16[208,256]{1,0:T(8,128)(2,1)}, bf16[49,4096]{1,0:T(8,128)(2,1)}, f32[208,1024]{1,0:T(8,128)}, bf16[32,16,512]{...) custom-call(s32[4]{0:T(128)} %pad_add_fusion.scal, ...), custom_call_target="tpu_custom_call" | custom-call | flops 12884901888 | bytes 62914560 | tf_op jit(solution)/shard_map/front/pallas_call | solution.py:760
  128.4 25.0 %dispatch.1.slots = bf16[4,32,16,512]{3,2,1,0:T(8,128)(2,1)} custom-call(bf16[32,16,512]{2,1,0:T(8,128)(2,1)} %get-tuple-element.27.src), custom_call_target="tpu_custom_call" | custom-call | bytes 41943040 | tf_op jit(solution)/shard_map/dispatch/pallas_call | solution.py:614
  153.3 10.7 %expert_bwd.1 = (bf16[1024,1024]{1,0:T(8,128)(2,1)}, bf16[1024,1024]{1,0:T(8,128)(2,1)}, bf16[4,32,16,512]{3,2,1,0:T(8,128)(2,1)}) custom-call(bf16[4,32,16,512]{3,2,1,0:T(8,128)(2,1)} %dispatch.1.slots, bf16[1024,1024]{1,0:T(8,128)(2,1)} %get-tuple-element.28.slope, bf16[4,1024,256]{2,1,0:T(8,128)(2,1)} %get-tuple-element.29.ups, ...), custom_call_target="tpu_custom_call" | custom-call | flops 4294967296 | bytes 14680064 | tf_op jit(solution)/shard_map/expert_bwd/pallas_call | solution.py:799
  164.1 35.4 %combine.1.ret = bf16[2,32,16,512]{3,2,1,0:T(8,128)(2,1)} custom-call(bf16[4,32,16,512]{3,2,1,0:T(8,128)(2,1)} %get-tuple-element.31.part), custom_call_target="tpu_custom_call" | custom-call | bytes 41943040 | tf_op jit(solution)/shard_map/combine/pallas_call | solution.py:678
  199.5 3.3 %after_back.1 = (f32[208,1024]{1,0:T(8,128)}, bf16[208,1024]{1,0:T(8,128)(2,1)}) custom-call(bf16[208,1024]{1,0:T(8,128)(2,1)} %get-tuple-element.26.after, bf16[2,32,16,512]{3,2,1,0:T(8,128)(2,1)} %combine.1.ret, bf16[208,256]{1,0:T(8,128)(2,1)} %get-tuple-element.32.table, f32[208,1024]{1,0:T(8,128)} %get-tuple-element.33.d_block), custom_call_target="tpu_custom_call" | custom-call | flops 1073741824 | bytes 4194304 | tf_op jit(solution)/shard_map/after_back/pallas_call | solution.py:718
  202.8 0.9 slice.44
  203.8 8.7 %expert_grads.1 = (bf16[4,256,1024]{2,1,0:T(8,128)(2,1)}, bf16[4,1024,256]{2,1,0:T(8,128)(2,1)}) custom-call(bf16[1024,1024]{1,0:T(8,128)(2,1)} %get-tuple-element.38.act, bf16[1024,1024]{1,0:T(8,128)(2,1)} %get-tuple-element.39.d_rows, bf16[1024,1024]{1,0:T(8,128)(2,1)} %get-tuple-element.40.rows, bf16[1024,1024]{1,0:T(8,128)(2,1)} %get-tuple-element.41.d_pre), custom_call_target="tpu_custom_call" | custom-call | flops 4294967296 | bytes 14680064 | tf_op jit(solution)/shard_map/expert_grads/pallas_call | solution.py:812
  212.5 2.7 slice_bitcast_fusion.4
  216.0 1.4 collective-permute-start.3
  217.4 1.9 collective-permute-start.2
  219.9 19.7 %attn_bwd.1.own = bf16[208,1024]{1,0:T(8,128)(2,1)} custom-call(s32[4]{0:T(128)} %pad_add_fusion.scal, bf16[208,1024]{1,0:T(8,128)(2,1)} %get-tuple-element.35.own, bf16[96,1024]{1,0:T(8,128)(2,1)} %copy-done.11, bf16[1024,3072]{1,0:T(8,128)(2,1)} %wv.1, bf16[1024,3072]{1,0:T(8,128)(2,1)} %wv.1, bf16[1024,3072]{1,0:T(8,128)(2,1)} %wv.1, ...), custom_call_target="tpu_custom_call" | custom-call | flops 8589934592 | bytes 14680064 | tf_op jit(solution)/shard_map/attn_bwd/pallas_call | solution.py:830
  239.6 0.9 slice.57
  240.7 1.3 slice_bitcast_fusion
  242.2 5.8 %collective-permute-done.1.halo = bf16[96,1024]{1,0:T(8,128)(2,1)S(1)} collective-permute-done((bf16[96,1024]{1,0:T(8,128)(2,1)S(1)}, bf16[96,1024]{1,0:T(8,128)(2,1)S(1)}, u32[]{:S(2)}, u32[]{:S(2)}) %collective-permute-start.1) | collective-permute-done | bytes 196640 | tf_op jit(solution)/shard_map/ppermute | solution.py:699
  248.0 1.0 collective-permute-start.6
  249.6 2.8 finish.1
  252.4 1.0 slice.58
  254.3 16.0 %collective-permute-done.7.refs_7_ = bf16[256,1024]{1,0:T(8,128)(2,1)S(1)} collective-permute-done((bf16[256,1024]{1,0:T(8,128)(2,1)}, bf16[256,1024]{1,0:T(8,128)(2,1)S(1)}, u32[]{:S(2)}, u32[]{:S(2)}) %collective-permute-start.7) | collective-permute-done | bytes 524320 | tf_op jit(solution)/shard_map/ppermute | solution.py:704
  271.3 5.7 %place_grads.1 = (f32[4,1024,256]{2,1,0:T(8,128)}, f32[4,256,1024]{2,1,0:T(8,128)}) custom-call(s32[1]{0:T(128)} %bitcast.1.turn, bf16[1024,256]{1,0:T(8,128)(2,1)} %get-tuple-element.57.refs_0_, bf16[1024,256]{1,0:T(8,128)(2,1)} %copy-done.5, bf16[1024,256]{1,0:T(8,128)(2,1)} %copy-done.4, bf16[1024,256]{1,0:T(8,128)(2,1)} %copy-done.3, ...), custom_call_target="tpu_custom_call" | custom-call | bytes 12582912 | tf_op jit(solution)/shard_map/place_grads/pallas_call | solution.py:854
  277.0 3.8 %fusion.2 = bf16[8,49,256]{2,1,0:T(8,128)(2,1)S(1)} fusion(bf16[8,49,4096]{2,1,0:T(8,128)(2,1)} %all-gather.4.cloned.1.call-done, bf16[4096,256]{1,0:T(8,128)(2,1)} %reduce_weight.1), kind=kOutput, calls=%fused_computation.3 | convolution fusion | flops 822183936 | bytes 5509120 | tf_op jit(solution)/shard_map/nkc,cd->nkd/dot_general | solution.py:849
  (52 shorter events, 11.5 us)
Async XLA Ops:
  7.2 7.4 %copy-start = (f32[32,169]{1,0:T(8,128)S(1)}, f32[32,169]{1,0:T(8,128)}, u32[]{:S(2)}) copy-start(f32[32,169]{1,0:T(8,128)} %param.15) | copy-start | bytes 64900
  7.2 269.9 %all-gather.4.cloned.1.call-start = ((), (), s32[]{:S(2)}) async-start(), calls=%async_computation | async-start | bytes 4128768 | tf_op jit(solution)/shard_map/all_gather | solution.py:850
  10.5 7.9 %copy-start.9 = (s32[208]{0:T(256)}, s32[208]{0:T(256)S(1)}, u32[]{:S(2)}) copy-start(s32[208]{0:T(256)S(1)} %pad.17) | copy-start | bytes 2500
  14.6 5.9 %copy-start.10 = (s32[2]{0:T(128)S(1)}, s32[2]{0:T(128)}, u32[]{:S(2)}) copy-start(s32[2]{0:T(128)} %param.16) | copy-start | bytes 28
  203.7 15.5 %collective-permute-start = (bf16[96,1024]{1,0:T(8,128)(2,1)S(1)}, bf16[96,1024]{1,0:T(8,128)(2,1)S(1)}, u32[]{:S(2)}, u32[]{:S(2)}) collective-permute-start(bf16[96,1024]{1,0:T(8,128)(2,1)S(1)} %slice.44), channel_id=1, source_target_pairs={{0,15},{1,0},{2,1},{3,2},{4,3},{5,4},{6,5},{7,6},{8,7},{9,8},{10,9... | collective-permute-start | bytes 589832 | tf_op jit(solution)/shard_map/ppermute | solution.py:699
  215.2 33.7 %collective-permute-start.4 = (bf16[1024,256]{1,0:T(8,128)(2,1)S(1)}, bf16[1024,256]{1,0:T(8,128)(2,1)S(1)}, u32[]{:S(2)}, u32[]{:S(2)}) collective-permute-start(bf16[1024,256]{1,0:T(8,128)(2,1)S(1)} %get-tuple-element.54), channel_id=1, source_target_pairs={{0,4},{1,5},{2,6},{3,7},{4,8},{5,9},{6,10},{7,11},{8,12},{9,13},{1... | collective-permute-start | bytes 1572872 | tf_op jit(solution)/shard_map/ppermute | solution.py:704
  216.0 38.3 %collective-permute-start.3 = (bf16[1024,256]{1,0:T(8,128)(2,1)}, bf16[1024,256]{1,0:T(8,128)(2,1)S(1)}, u32[]{:S(2)}, u32[]{:S(2)}) collective-permute-start(bf16[1024,256]{1,0:T(8,128)(2,1)} %get-tuple-element.55), channel_id=1, source_target_pairs={{0,8},{1,9},{2,10},{3,11},{4,12},{5,13},{6,14},{7,15},{8,0},{9,1},... | collective-permute-start | bytes 1572872 | tf_op jit(solution)/shard_map/ppermute | solution.py:704
  217.4 36.9 %collective-permute-start.2 = (bf16[1024,256]{1,0:T(8,128)(2,1)}, bf16[1024,256]{1,0:T(8,128)(2,1)S(1)}, u32[]{:S(2)}, u32[]{:S(2)}) collective-permute-start(bf16[1024,256]{1,0:T(8,128)(2,1)} %get-tuple-element.56), channel_id=1, source_target_pairs={{0,12},{1,13},{2,14},{3,15},{4,0},{5,1},{6,2},{7,3},{8,4},{9,5},{1... | collective-permute-start | bytes 1572872 | tf_op jit(solution)/shard_map/ppermute | solution.py:704
  219.2 0.7 copy-start.11
  219.9 20.7 %copy-start.2 = (bf16[4,256,1024]{2,1,0:T(8,128)(2,1)S(1)}, bf16[4,256,1024]{2,1,0:T(8,128)(2,1)}, u32[]{:S(2)}) copy-start(bf16[4,256,1024]{2,1,0:T(8,128)(2,1)} %get-tuple-element.43) | copy-start | bytes 6291460
  240.6 7.4 %collective-permute-start.1 = (bf16[96,1024]{1,0:T(8,128)(2,1)S(1)}, bf16[96,1024]{1,0:T(8,128)(2,1)S(1)}, u32[]{:S(2)}, u32[]{:S(2)}) collective-permute-start(bf16[96,1024]{1,0:T(8,128)(2,1)S(1)} %slice.57), channel_id=1, source_target_pairs={{0,1},{1,2},{2,3},{3,4},{4,5},{5,6},{6,7},{7,8},{8,9},{9,10},{10,1... | collective-permute-start | bytes 589832 | tf_op jit(solution)/shard_map/ppermute | solution.py:699
  242.0 28.3 %collective-permute-start.7 = (bf16[256,1024]{1,0:T(8,128)(2,1)}, bf16[256,1024]{1,0:T(8,128)(2,1)S(1)}, u32[]{:S(2)}, u32[]{:S(2)}) collective-permute-start(bf16[256,1024]{1,0:T(8,128)(2,1)} %get-tuple-element.50), channel_id=1, source_target_pairs={{0,4},{1,5},{2,6},{3,7},{4,8},{5,9},{6,10},{7,11},{8,12},{9,13},{1... | collective-permute-start | bytes 1572872 | tf_op jit(solution)/shard_map/ppermute | solution.py:704
  248.0 1.6 copy-start.8
  248.0 22.4 %collective-permute-start.6 = (bf16[256,1024]{1,0:T(8,128)(2,1)}, bf16[256,1024]{1,0:T(8,128)(2,1)S(1)}, u32[]{:S(2)}, u32[]{:S(2)}) collective-permute-start(bf16[256,1024]{1,0:T(8,128)(2,1)} %get-tuple-element.51), channel_id=1, source_target_pairs={{0,8},{1,9},{2,10},{3,11},{4,12},{5,13},{6,14},{7,15},{8,0},{9,1},... | collective-permute-start | bytes 1572872 | tf_op jit(solution)/shard_map/ppermute | solution.py:704
  248.9 21.4 %copy-start.3 = (bf16[1024,256]{1,0:T(8,128)(2,1)}, bf16[1024,256]{1,0:T(8,128)(2,1)S(1)}, u32[]{:S(2)}) copy-start(bf16[1024,256]{1,0:T(8,128)(2,1)S(1)} %collective-permute-done.4.refs_3_) | copy-start | bytes 1572868
  248.9 21.4 %collective-permute-start.5 = (bf16[256,1024]{1,0:T(8,128)(2,1)}, bf16[256,1024]{1,0:T(8,128)(2,1)}, u32[]{:S(2)}, u32[]{:S(2)}) collective-permute-start(bf16[256,1024]{1,0:T(8,128)(2,1)} %get-tuple-element.52), channel_id=1, source_target_pairs={{0,12},{1,13},{2,14},{3,15},{4,0},{5,1},{6,2},{7,3},{8,4},{9,5},{1... | collective-permute-start | bytes 1572872 | tf_op jit(solution)/shard_map/ppermute | solution.py:704
  254.3 16.1 %copy-start.4 = (bf16[1024,256]{1,0:T(8,128)(2,1)}, bf16[1024,256]{1,0:T(8,128)(2,1)S(1)}, u32[]{:S(2)}) copy-start(bf16[1024,256]{1,0:T(8,128)(2,1)S(1)} %collective-permute-done.3.refs_2_) | copy-start | bytes 1572868
  254.3 16.1 %copy-start.5 = (bf16[1024,256]{1,0:T(8,128)(2,1)}, bf16[1024,256]{1,0:T(8,128)(2,1)S(1)}, u32[]{:S(2)}) copy-start(bf16[1024,256]{1,0:T(8,128)(2,1)S(1)} %collective-permute-done.2.refs_1_) | copy-start | bytes 1572868
  270.3 0.8 copy-start.6
  270.3 1.0 copy-start.7
  277.0 4.6 %copy-start.1 = (f32[32,169]{1,0:T(8,128)S(1)}, f32[32,169]{1,0:T(8,128)}, u32[]{:S(2)}) copy-start(f32[32,169]{1,0:T(8,128)} %param.15) | copy-start | bytes 64900
Sparse Core Ops, SparseCore 0:
  128.5 87.4 all-gather.3
